TPU v7x, 128 devices: a whole 4x4x4 slice. The times are simulated.
128 devices in a mesh: dp: 16 (over x, z_lo, core), tensor: 8 (over z_hi, y).
Axes of the slice: x: 4, y: 4, z: 4 (z_hi: 2, z_lo: 2; z = z_hi * 2 + z_lo), core: 2. Of those that a mesh axis runs over, the one named last changes fastest.
Arguments:
- layer_input: bfloat16 [64, 256, 4096], P('dp', None, 'tensor'), may hold values from -6 to 6
- output_cotangent: bfloat16 [64, 256, 4096], P('dp'), may hold values from -6 to 6
- gate_preact: bfloat16 [64, 256, 14336], P('dp', None, 'tensor'), may hold values from -8 to 8
- down_weight: bfloat16 [14336, 4096], P('tensor', 'dp'), may hold values from -0.046875 to 0.046875
- lengths: int32 [64], P('dp'), may hold values from 32 to 256, as said below
- input_signs: int32 [4096, 8], P('tensor'), may hold values from 0 to 1
- hidden_signs: int32 [14336, 8], P('tensor'), may hold values from 0 to 1
- basis_in: float32 [8, 8], replicated, may hold values from -2 to 2
- basis_out: float32 [8, 8], replicated, may hold values from -2 to 2
- eigenvalues: float32 [8, 8], replicated, may hold values from 0.05 to 5
- query_grads: float32 [4096, 64], P('tensor', 'dp'), may hold values from -6 to 6
Outputs:
- scores: float32 [64, 4096], P('dp', 'tensor')
Inputs may be any that keep to these rules, and one draw needn't show every extreme that they name: `lengths`: some example has all 256 tokens.
All inputs are finite; a program needn't handle non-finite values.
Results may differ from a plain program's by a relative error of at most 0.003.
Values may be sent and summed in bfloat16 or wider, within the bound.
A program may use at most 256 MiB of HBM per device.

v0:
```python
import jax
import jax.numpy as jnp
from jax import lax
from jax.sharding import PartitionSpec as P

D = 4096
FF = 14336
RA = 8
RG = 8


damping_shift = 0.1


def on_device(
    layer_input,
    output_cotangent,
    gate_preact,
    down_weight,
    lengths,
    input_signs,
    hidden_signs,
    basis_in,
    basis_out,
    eigenvalues,
    query_grads,
):
    examples = layer_input.shape[0]
    slots = layer_input.shape[1]
    tok_rows = examples * slots
    hid_local = gate_preact.shape[2]
    inputs = layer_input.reshape(tok_rows, layer_input.shape[2])
    cotangent = output_cotangent.reshape(tok_rows, output_cotangent.shape[2])
    gate = gate_preact.reshape(tok_rows, hid_local)
    sign_in = (2 * input_signs - 1).astype(jnp.bfloat16)
    sign_hid = (2 * hidden_signs - 1).astype(jnp.bfloat16)
    input_proj = jnp.dot(inputs, sign_in, preferred_element_type=jnp.float32) * D ** (-0.5)
    contract = (((1,), (1,)), ((), ()))
    hidden_grad = lax.dot_general(
        cotangent,
        lax.all_gather(down_weight, "dp", axis=1, tiled=True),
        contract,
        preferred_element_type=jnp.float32,
    )
    up_grad = (hidden_grad * jax.nn.silu(gate.astype(jnp.float32))).astype(jnp.bfloat16)
    output_proj = jnp.dot(up_grad, sign_hid, preferred_element_type=jnp.float32) * FF ** (-0.5)
    stacked = jnp.concatenate([input_proj, output_proj], axis=1)
    counts = lengths.astype(jnp.float32)
    summed = lax.psum(stacked, "tensor")
    in_full = summed[:, :RA].reshape(examples, slots, RA)
    out_full = summed[:, RA:].reshape(examples, slots, RG)
    positions = jnp.arange(slots, dtype=jnp.int32)
    weight = (positions[None, :] < lengths[:, None]).astype(jnp.float32) / counts[:, None]
    example_grad = jnp.einsum(
        "et,eta,etb->eab", weight, in_full, out_full, precision=lax.Precision.HIGHEST
    )
    rotated = jnp.einsum(
        "ai,eab,bj->eij", basis_in, example_grad, basis_out, precision=lax.Precision.HIGHEST
    )
    full_queries = lax.all_gather(query_grads, "dp", axis=1, tiled=True)
    queries = full_queries.reshape(full_queries.shape[0], RA, RG)
    precond = jnp.einsum(
        "ai,qab,bj->qij", basis_in, queries, basis_out, precision=lax.Precision.HIGHEST
    ) / (eigenvalues + damping_shift)
    return jnp.einsum("eij,qij->eq", rotated, precond, precision=lax.Precision.HIGHEST)


def solution(mesh):
    in_specs = (
        P("dp", None, "tensor"),
        P("dp", None, None),
        P("dp", None, "tensor"),
        P("tensor", "dp"),
        P("dp"),
        P("tensor", None),
        P("tensor", None),
        P(),
        P(),
        P(),
        P("tensor", "dp"),
    )
    out_specs = P("dp", "tensor")
    return jax.shard_map(
        on_device, mesh=mesh, in_specs=in_specs, out_specs=out_specs, check_vma=False
    )
```

profile of v0, /device:TPU:0, one launch (start us, length us, event | category | flops | bytes accessed | tf_op | source)
XLA Modules:
  0.0 219.3 jit_solution(11366496863435062079)
XLA Ops:
  6.5 0.0 copy-start
  6.5 0.0 all-gather.3.cloned.1.call-start
  6.5 0.7 all-gather.3.cloned.1.call-update
  7.3 0.0 all-reduce.2.cloned.1.call-start
  7.3 0.7 convert_element_type.22
  8.0 20.9 %all-gather = f32[16,4,512]{2,1,0:T(4,128)S(1)} all-gather(f32[1,4,512]{2,1,0:T(4,128)} %bitcast.40), channel_id=1, replica_groups=mesh['dp'=16,'tensor'=8] {'dp'}, dimensions={0}, use_global_device_ids=true | all-gather | bytes 139264 | tf_op jit(solution)/shard_map/all_gather | solution.py:60
  28.9 0.7 broadcast_add_fusion
  29.6 1.0 fusion.9
  30.6 1.0 convolution_divide_fusion
  31.6 0.0 copy-done
  31.7 1.1 fusion.7
  32.7 67.9 %all-gather.3.cloned.1.call-done = bf16[1792,4096]{1,0:T(8,128)(2,1)} async-done(((bf16[1792,256]{1,0:T(8,128)(2,1)}), bf16[1792,4096]{1,0:T(8,128)(2,1)}) %all-gather.3.cloned.1.call-update) | async-done | bytes 14680080 | tf_op jit(solution)/shard_map/all_gather | solution.py:41
  100.7 0.0 copy-start.3
  100.7 0.0 copy-start.1
  100.7 0.0 copy-start.2
  100.7 24.7 %fusion.6 = f32[1024,8]{0,1:T(8,128)S(1)} fusion(bf16[1024,1792]{1,0:T(8,128)(2,1)} %bitcast.42, bf16[1024,4096]{1,0:T(8,128)(2,1)} %bitcast.41, bf16[1792,4096]{1,0:T(8,128)(2,1)} %all-gather.3.cloned.1.call-done, s32[1792,8]{0,1:T(8,128)} %param.17), kind=kOutput, calls=%fused_computation.9 | convolution fusion | flops 15074641920 | bytes 26828800 | tf_op jit(solution)/shard_map/dot_general | solution.py:46
  125.4 0.7 pad_maximum_fusion
  126.0 0.0 all-reduce.2.cloned.1.call-update
  126.1 0.0 copy-done.3
  126.1 0.1 convert_divide_fusion
  126.2 84.1 %all-reduce.2.cloned.1.call-done = f32[1024,16]{0,1:T(8,128)} async-done(((f32[1024,16]{0,1:T(8,128)}), f32[1024,16]{0,1:T(8,128)}) %all-reduce.2.cloned.1.call-update) | async-done | bytes 65552 | tf_op jit(solution)/shard_map/psum | solution.py:49
  210.3 0.8 fusion.29
  211.0 0.2 fusion.11
  211.2 0.0 copy-done.1
  211.2 0.1 fusion.22
  211.3 0.1 copy.24
  211.4 0.0 copy-done.2
  211.4 0.2 fusion.19
  211.6 0.9 convolution_bitcast_fusion
  (1 shorter events, 0.0 us)
Async XLA Ops:
  6.5 25.1 %copy-start = (bf16[4,256,512]{2,1,0:T(8,128)(2,1)S(1)}, bf16[4,256,512]{2,1,0:T(8,128)(2,1)}, u32[]{:S(2)}) copy-start(bf16[4,256,512]{2,1,0:T(8,128)(2,1)} %param.11) | copy-start | bytes 3145732
  6.5 94.1 %all-gather.3.cloned.1.call-start = ((), (), s32[]{:S(2)}) async-start(), calls=%async_computation | async-start | bytes 15597568 | tf_op jit(solution)/shard_map/all_gather | solution.py:41
  7.3 203.0 %all-reduce.2.cloned.1.call-start = ((), (), s32[]{:S(2)}) async-start(), calls=%async_computation.1 | async-start | bytes 131072 | tf_op jit(solution)/shard_map/psum | solution.py:49
  100.7 25.4 %copy-start.3 = (s32[4]{0:T(128)S(1)}, s32[4]{0:T(128)}, u32[]{:S(2)}) copy-start(s32[4]{0:T(128)} %param.15) | copy-start | bytes 52
  100.7 110.5 %copy-start.1 = (f32[8,8]{1,0:T(8,128)S(1)}, f32[8,8]{1,0:T(8,128)}, u32[]{:S(2)}) copy-start(f32[8,8]{1,0:T(8,128)} %param.18) | copy-start | bytes 772
  100.7 110.8 %copy-start.2 = (f32[8,8]{1,0:T(8,128)S(1)}, f32[8,8]{1,0:T(8,128)}, u32[]{:S(2)}) copy-start(f32[8,8]{1,0:T(8,128)} %param.19) | copy-start | bytes 772
Sparse Core Ops, SparseCore 0:
  9.0 91.6 all-gather.2
  126.2 84.0 all-reduce.1
where the time goes:
time: 220 us; the launch traced here: 219 us
  waiting for transfers between devices  153 us (70%)
  matrix products  29.2 us (13%)
  blocking collectives  20.9 us (10%)
  between operations  13.5 us (6%)
    psum x1, waiting for transfers between devices, on_device(): summed = lax.psum(stacked, 'tensor')  84.1 us
    all_gather x1, waiting for transfers between devices, on_device(): lax.all_gather(down_weight, 'dp', axis=1, tiled=True)  67.9 us
    dot_general x1, matrix products, on_device(): jnp.dot(up_grad, sign_hid, preferred_element_type=jnp.float32)  24.7 us
    all_gather x1, blocking collectives, on_device(): full_queries = lax.all_gather(query_grads, 'dp', axis=1, tiled=True)  20.9 us
  transfers between devices with their start and end apart: 2, of which 2 were waited for; matrix products, arithmetic and copies ran while one was open for 2% of the time, Pallas kernels for 0%

commit v1 on v0

v1 whole, which is shorter than its diff:
```python
import functools

import jax
import jax.numpy as jnp
from jax import lax
from jax.experimental import pallas as pl
from jax.experimental.pallas import tpu as pltpu
from jax.sharding import PartitionSpec as P

MESH = pl.DeviceIdType.MESH
HIGH = lax.Precision.HIGHEST
F32, BF16 = jnp.float32, jnp.bfloat16
D, FF, RA, RG = 4096, 14336, 8, 8
SHIFT = 0.1
TOK, HID, COLS, SLOTS = 1024, 1792, 256, 256
BLOCK = 256
NT = (((1,), (1,)), ((), ()))

STAGES = [(256 * i, 256, "abcabd"[i]) for i in range(6)]
STAGES += [(1536, 96, "a"), (1632, 80, "b"), (1712, 80, "c")]
N = len(STAGES)
O, L, R, Z, FAR, ZL, ZR, ZF = range(8)
HOP2 = {
    "a": ((L, "xp", FAR), (Z, "xp", ZL), (Z, "xm", ZR)),
    "b": ((R, "xm", FAR), (Z, "xm", ZR), (Z, "xp", ZL)),
    "c": ((L, "xp", FAR), (Z, "xm", ZR), (L, "z", ZL)),
    "d": ((R, "xm", FAR), (Z, "xp", ZL), (R, "z", ZR)),
}
HOP1 = ((O, "xp", L), (O, "xm", R), (O, "z", Z))


def column(slot, sibling=0):
    return (slot // 4) * 2048 + sibling * 1024 + (slot % 4) * COLS


def kernel(
    li_hbm, ct_hbm, gate_hbm, w_hbm, len_ref, sin_hbm, shid_hbm, bi_hbm, bo_hbm, ev_hbm, q_hbm,
    o_ref,
    w, ct, gate, li, sin, shid, bi, bo, ev, qbuf, qfull, mat, ybuf, zbuf, gbuf, in64, s64, hid, out64,
    ss_w, rs_w, ss_s, rs_s, ss_q, rs_q, ss_y, rs_y, ss_z, rs_z, ss_g, rs_g, lsem,
):
    dp, tn = lax.axis_index("dp"), lax.axis_index("tensor")
    x, z, c = dp // 4, (dp // 2) % 2, dp % 2
    zh, y = tn // 4, tn % 4
    xp, xm = (x + 1) % 4, (x + 3) % 4
    at = lambda xx, zz, cc: xx * 4 + zz * 2 + cc
    dev = {
        "xp": (at(xp, z, c), tn),
        "xm": (at(xm, z, c), tn),
        "z": (at(x, 1 - z, c), tn),
        "sib": (at(x, z, 1 - c), tn),
    }

    loads = []

    def load(src, dst):
        cp = pltpu.make_async_copy(src, dst, lsem.at[len(loads)])
        loads.append(cp)
        cp.start()
        return cp

    own = [load(w_hbm.at[pl.ds(0, 512)], w.at[pl.ds(0, 512), pl.ds(0, COLS)])]
    own += [load(w_hbm.at[pl.ds(512, 1280)], w.at[pl.ds(512, 1280), pl.ds(0, COLS)])]

    barrier = pltpu.get_barrier_semaphore()
    for i in range(1, 16):
        pl.semaphore_signal(barrier, inc=1, device_id=((dp + i) % 16, tn), device_id_type=MESH)
    for i in range(1, 8):
        pl.semaphore_signal(barrier, inc=1, device_id=(dp, (tn + i) % 8), device_id_type=MESH)

    load_li = load(li_hbm, li)
    load_sin = load(sin_hbm, sin)
    load_q = load(q_hbm, qbuf.at[dp])
    load_small = [load(bi_hbm, bi), load(bo_hbm, bo), load(ev_hbm, ev), load(shid_hbm, shid)]
    load_c = []
    for half in range(2):
        cc = c if half == 0 else 1 - c
        for slot, (xx, zz) in enumerate(
            ((x, z), (xm, z), (xp, z), (x, 1 - z), ((x + 2) % 4, z), (xm, 1 - z), (xp, 1 - z), ((x + 2) % 4, 1 - z))
        ):
            first = pl.multiple_of(at(xx, zz, cc) * COLS, COLS)
            load_c.append(load(ct_hbm.at[:, pl.ds(first, COLS)], ct.at[:, pl.ds(column(slot, half), COLS)]))
    load_gate = load(gate_hbm, gate)

    pl.semaphore_wait(barrier, 22)

    def piece(stage, slot):
        first, rows, _ = STAGES[stage]
        return w.at[pl.ds(first, rows), pl.ds(column(slot), COLS)]

    sent = []

    def send(stage, src, to, dst):
        cp = pltpu.make_async_remote_copy(
            src_ref=piece(stage, src), dst_ref=piece(stage, dst),
            send_sem=ss_w.at[stage, dst], recv_sem=rs_w.at[stage, dst],
            device_id=dev[to], device_id_type=MESH,
        )
        cp.start()
        sent.append(cp)

    def arrive(stage, slot):
        pltpu.make_async_remote_copy(
            src_ref=piece(stage, slot), dst_ref=piece(stage, slot),
            send_sem=ss_w.at[stage, slot], recv_sem=rs_w.at[stage, slot],
            device_id=dev["z"], device_id_type=MESH,
        ).wait_recv()

    def share_copy(stage, group):
        first, rows, _ = STAGES[stage]
        return pltpu.make_async_remote_copy(
            src_ref=w.at[pl.ds(first, rows), pl.ds(group * 2048, 1024)],
            dst_ref=w.at[pl.ds(first, rows), pl.ds(group * 2048 + 1024, 1024)],
            send_sem=ss_s.at[stage, group], recv_sem=rs_s.at[stage, group],
            device_id=dev["sib"], device_id_type=MESH,
        )

    def share(stage, group):
        cp = share_copy(stage, group)
        cp.start()
        sent.append(cp)

    def shared(stage, group):
        share_copy(stage, group).wait_recv()

    def hop1(stage):
        for src, to, dst in HOP1:
            send(stage, src, to, dst)

    row8 = lax.broadcasted_iota(jnp.int32, (8, 64), 0)
    col8 = lax.broadcasted_iota(jnp.int32, (8, 64), 1)
    by_b = (col8 % 8 == row8).astype(F32)
    by_a = (col8 // 8 == row8).astype(F32)
    row64 = lax.broadcasted_iota(jnp.int32, (64, 8), 0)
    col64 = lax.broadcasted_iota(jnp.int32, (64, 8), 1)
    by_b_t = (row64 % 8 == col64).astype(F32)
    by_a_t = (row64 // 8 == col64).astype(F32)
    dot = functools.partial(jnp.dot, precision=HIGH, preferred_element_type=F32)

    q_sent, y_sent, z_sent = [], [], []

    def send_queries():
        for i in range(1, 16):
            cp = pltpu.make_async_remote_copy(
                src_ref=q_hbm, dst_ref=qbuf.at[dp], send_sem=ss_q.at[i], recv_sem=rs_q.at[dp],
                device_id=((dp + i) % 16, tn), device_id_type=MESH,
            )
            cp.start()
            q_sent.append(cp)

    def input_part():
        load_li.wait()
        load_sin.wait()
        sign = (2 * sin[...] - 1).astype(F32).astype(BF16)
        ybuf[y] = lax.dot_general(sign, li[...], NT, preferred_element_type=F32) * D ** (-0.5)
        for i in range(1, 4):
            cp = pltpu.make_async_remote_copy(
                src_ref=ybuf.at[y], dst_ref=ybuf.at[y], send_sem=ss_y.at[i], recv_sem=rs_y.at[y],
                device_id=(dp, zh * 4 + (y + i) % 4), device_id_type=MESH,
            )
            cp.start()
            y_sent.append(cp)

    def input_sum():
        for i in range(1, 4):
            other = (y + i) % 4
            pltpu.make_async_remote_copy(
                src_ref=ybuf.at[other], dst_ref=ybuf.at[other], send_sem=ss_y.at[i], recv_sem=rs_y.at[other],
                device_id=(dp, tn), device_id_type=MESH,
            ).wait_recv()
        zbuf[zh] = ybuf[0] + ybuf[1] + ybuf[2] + ybuf[3]
        cp = pltpu.make_async_remote_copy(
            src_ref=zbuf.at[zh], dst_ref=zbuf.at[zh], send_sem=ss_z, recv_sem=rs_z,
            device_id=(dp, (1 - zh) * 4 + y), device_id_type=MESH,
        )
        cp.start()
        z_sent.append(cp)

    def input_weigh():
        other = 1 - zh
        pltpu.make_async_remote_copy(
            src_ref=zbuf.at[other], dst_ref=zbuf.at[other], send_sem=ss_z, recv_sem=rs_z,
            device_id=(dp, other * 4 + y), device_id_type=MESH,
        ).wait_recv()
        full = zbuf[0] + zbuf[1]
        pos = lax.broadcasted_iota(jnp.int32, (8, SLOTS), 1)
        for e in range(TOK // SLOTS):
            count = len_ref[e]
            scale = FF ** (-0.5) / count.astype(F32)
            part = full[:, e * SLOTS : (e + 1) * SLOTS]
            part = jnp.where(pos < count, part * scale, 0.0)
            in64[pl.ds(e * SLOTS, SLOTS), :] = dot(part.T, by_a)

    def hidden_signs():
        load_small[3].wait()
        sign = (2 * shid[...] - 1).astype(F32)
        s64[...] = jnp.dot(by_b_t.astype(BF16), sign.astype(BF16), preferred_element_type=F32).astype(BF16)

    def query_matrix():
        for cp in load_small[:3]:
            cp.wait()
        load_q.wait()
        for i in range(1, 16):
            other = (dp + i) % 16
            pltpu.make_async_remote_copy(
                src_ref=q_hbm, dst_ref=qbuf.at[other], send_sem=ss_q.at[i], recv_sem=rs_q.at[other],
                device_id=(dp, tn), device_id_type=MESH,
            ).wait_recv()
        for i in range(16):
            qfull[pl.ds(4 * i, 4), :] = qbuf[i]
        kron = dot(dot(by_a_t, bi[...]), by_a) * dot(dot(by_b_t, bo[...]), by_b)
        values = jnp.sum(dot(ev[...], by_b) * by_a, axis=0, keepdims=True)
        both = lax.dot_general(kron / (values + SHIFT), kron, NT, precision=HIGH, preferred_element_type=F32)
        mat[...] = jnp.zeros_like(mat)
        mat[pl.ds(0, 64), :] = dot(both, qfull[...])

    def finish(j, product):
        cols = pl.ds(j * BLOCK, BLOCK)
        g = gate[:, cols].astype(F32)
        up = (product * (g * (0.5 + 0.5 * jnp.tanh(0.5 * g)))).astype(BF16)
        part = lax.dot_general(up, s64[:, cols], NT, preferred_element_type=F32)
        if j == 0:
            out64[...] = part
        else:
            out64[...] += part

    def block(j):
        if j == 0:
            for cp in load_c:
                cp.wait()
            load_gate.wait()
        shared(j, 0)
        shared(j, 1)
        finish(j, lax.dot_general(ct[...], w[pl.ds(j * BLOCK, BLOCK), :], NT, preferred_element_type=F32))

    last = HID // BLOCK - 1
    last_rows = pl.ds(last * BLOCK, BLOCK)

    own[0].wait()
    hop1(0)
    hop1(1)
    own[1].wait()
    for k in range(N + 3):
        if k > 0 and k + 1 < N:
            hop1(k + 1)
        if k < N:
            for slot in (L, R, Z):
                arrive(k, slot)
            for src, to, dst in HOP2[STAGES[k][2]]:
                send(k, src, to, dst)
            share(k, 0)
        if 0 <= k - 1 < N:
            for slot in (FAR, ZL, ZR):
                arrive(k - 1, slot)
            send(k - 1, FAR, "z", ZF)
        if 0 <= k - 2 < N:
            arrive(k - 2, ZF)
            share(k - 2, 1)
        if k == 0:
            send_queries()
            input_part()
            hidden_signs()
        if k == 1:
            input_sum()
        if k == 2:
            input_weigh()
            query_matrix()
        if 0 <= k - 3 < last:
            block(k - 3)
        if k == N:
            for s in range(last, N):
                shared(s, 0)
            hid[...] = lax.dot_general(
                ct[:, pl.ds(0, 2048)], w[last_rows, pl.ds(0, 2048)], NT, preferred_element_type=F32
            )
    for s in range(last, N):
        shared(s, 1)
    finish(
        last,
        hid[...]
        + lax.dot_general(
            ct[:, pl.ds(2048, 2048)], w[last_rows, pl.ds(2048, 2048)], NT, preferred_element_type=F32
        ),
    )

    rows = [
        jnp.sum(in64[pl.ds(e * SLOTS, SLOTS), :] * out64[pl.ds(e * SLOTS, SLOTS), :], axis=0, keepdims=True)
        for e in range(TOK // SLOTS)
    ]
    gbuf[tn] = jnp.zeros((8, 128), F32)
    for e in range(TOK // SLOTS):
        gbuf[tn, pl.ds(e, 1), pl.ds(0, 64)] = rows[e]
    g_sent = []
    for i in range(1, 8):
        cp = pltpu.make_async_remote_copy(
            src_ref=gbuf.at[tn], dst_ref=gbuf.at[tn], send_sem=ss_g.at[i], recv_sem=rs_g.at[tn],
            device_id=(dp, (tn + i) % 8), device_id_type=MESH,
        )
        cp.start()
        g_sent.append(cp)
    for cp in sent + q_sent + y_sent + z_sent:
        cp.wait_send()
    for i in range(1, 8):
        other = (tn + i) % 8
        pltpu.make_async_remote_copy(
            src_ref=gbuf.at[other], dst_ref=gbuf.at[other], send_sem=ss_g.at[i], recv_sem=rs_g.at[other],
            device_id=(dp, tn), device_id_type=MESH,
        ).wait_recv()
    total = gbuf[0]
    for i in range(1, 8):
        total = total + gbuf[i]
    o_ref[...] = dot(total, mat[...])[:4, :]
    for cp in g_sent:
        cp.wait_send()


def on_device(
    layer_input, output_cotangent, gate_preact, down_weight, lengths, input_signs, hidden_signs,
    basis_in, basis_out, eigenvalues, query_grads,
):
    any_spec = pl.BlockSpec(memory_space=pl.ANY)
    vmem, dma = pltpu.VMEM, pltpu.SemaphoreType.DMA
    specs = [any_spec] * 11
    specs[4] = pl.BlockSpec(memory_space=pltpu.SMEM)
    return pl.pallas_call(
        kernel,
        out_shape=jax.ShapeDtypeStruct((4, 512), F32),
        in_specs=specs,
        out_specs=pl.BlockSpec(memory_space=pltpu.VMEM),
        scratch_shapes=[
            vmem((HID, D), BF16),
            vmem((TOK, D), BF16),
            vmem((TOK, HID), BF16),
            vmem((TOK, 512), BF16),
            vmem((8, 512), jnp.int32),
            vmem((8, HID), jnp.int32),
            vmem((8, 8), F32),
            vmem((8, 8), F32),
            vmem((8, 8), F32),
            vmem((16, 4, 512), F32),
            vmem((64, 512), F32),
            vmem((128, 512), F32),
            vmem((4, 8, TOK), F32),
            vmem((2, 8, TOK), F32),
            vmem((8, 8, 128), F32),
            vmem((TOK, 64), F32),
            vmem((64, HID), BF16),
            vmem((TOK, BLOCK), F32),
            vmem((TOK, 64), F32),
            dma((N, 8)), dma((N, 8)), dma((N, 2)), dma((N, 2)), dma((16,)), dma((16,)),
            dma((4,)), dma((4,)), dma, dma, dma((8,)), dma((8,)), dma((32,)),
        ],
        compiler_params=pltpu.CompilerParams(
            collective_id=0, has_side_effects=True, vmem_limit_bytes=56 * 1024 * 1024
        ),
        cost_estimate=pl.CostEstimate(flops=2 * TOK * HID * D, bytes_accessed=30_000_000, transcendentals=TOK * HID),
        name="scores",
    )(
        layer_input.reshape(TOK, 512),
        output_cotangent.reshape(TOK, D),
        gate_preact.reshape(TOK, HID),
        down_weight,
        lengths,
        input_signs.T,
        hidden_signs.T,
        basis_in,
        basis_out,
        eigenvalues,
        query_grads.T,
    )


def solution(mesh):
    in_specs = (
        P("dp", None, "tensor"),
        P("dp", None, None),
        P("dp", None, "tensor"),
        P("tensor", "dp"),
        P("dp"),
        P("tensor", None),
        P("tensor", None),
        P(),
        P(),
        P(),
        P("tensor", "dp"),
    )
    return jax.shard_map(
        on_device, mesh=mesh, in_specs=in_specs, out_specs=P("dp", "tensor"), check_vma=False
    )
```

time: 220 us -> 86.4 us (0.39)
  waiting for transfers between devices: 153 us -> 0 us
  Pallas kernels: 0 us -> 83.5 us
  matrix products: 29.2 us -> 0 us
  blocking collectives: 20.9 us -> 0 us
  between operations: 13.5 us -> 0.01 us
    psum x1 -> x0, waiting for transfers between devices: 84.1 us -> none  [on_device(): summed = lax.psum(stacked, 'tensor')]
    pallas_call x0 -> x1, Pallas kernels: none -> 83.5 us  [on_device(): pl.pallas_call(kernel, out_shape=jax.ShapeDtypeStruct((4, 512), F32), in_...]
    all_gather x1 -> x0, waiting for transfers between devices: 67.9 us -> none  [on_device(): lax.all_gather(down_weight, 'dp', axis=1, tiled=True)]
    dot_general x8 -> x0, matrix products: 29.2 us -> none  [the longest x1 24.7 us: on_device(): jnp.dot(up_grad, sign_hid, preferred_element_type=jnp.float32)]
    all_gather x1 -> x0, blocking collectives: 20.9 us -> none  [on_device(): full_queries = lax.all_gather(query_grads, 'dp', axis=1, tiled=True)]
  transfers between devices with their start and end apart: 2 -> 0, of which waited for: 2 -> 0; matrix products, arithmetic and copies ran while one was open for 2% -> 0% of each run, Pallas kernels for 0% -> 0%
where the time goes in v1:
time: 86.4 us; the launch traced here: 84.8 us
  Pallas kernels  83.5 us (97%)
  local copies, waits for them, and re-layouts  1.3 us (2%)
    pallas_call x1, Pallas kernels, on_device(): pl.pallas_call(kernel, out_shape=jax.ShapeDtypeStruct((4, 512), F32), in_...  83.5 us

profile of v1, /device:TPU:0, one launch (start us, length us, event | category | flops | bytes accessed | tf_op | source)
XLA Modules:
  0.0 84.8 jit_solution(10132181106584936592)
XLA Ops:
  0.0 83.5 %scores.1 = f32[4,512]{1,0:T(4,128)} custom-call(bf16[1024,512]{1,0:T(8,128)(2,1)} %bitcast.8, bf16[1024,4096]{1,0:T(8,128)(2,1)} %bitcast.6, bf16[1024,1792]{1,0:T(8,128)(2,1)} %bitcast.7, bf16[1792,256]{1,0:T(8,128)(2,1)} %w_hbm.1, s32[4]{0:T(128)} %len_ref.1, s32[8,512]{1,0:T(8,128)} %bitcast.10, s32[8,1792]{1,0:T(8,128)} %bitcast.9, f32[8,8]{1,0:T(8,128)} %bi_hbm.1, ...), custom_call_target="tpu_custom_call" | custom-call | flops 15032385536 | bytes 30000000 | tf_op jit(solution)/shard_map/scores/pallas_call | solution.py:325
  83.5 1.3 %copy.13 = f32[4,512]{1,0:T(4,128)} copy(f32[4,512]{1,0:T(4,128)} %scores.1) | data formatting | bytes 16384

commit v2 on v1

--- a/solution.py
+++ b/solution.py
@@ -16,17 +16,38 @@
 BLOCK = 256
 NT = (((1,), (1,)), ((), ()))
 
-STAGES = [(256 * i, 256, "abcabd"[i]) for i in range(6)]
-STAGES += [(1536, 96, "a"), (1632, 80, "b"), (1712, 80, "c")]
-N = len(STAGES)
+SIZES = (256, 256, 256, 256, 256, 256, 128, 64, 64)
+N = len(SIZES)
+STAGES = [(sum(SIZES[:i]), rows) for i, rows in enumerate(SIZES)]
+LAST = HID // BLOCK - 1
+IN_LAST = [i for i, (first, _) in enumerate(STAGES) if first >= LAST * BLOCK]
 O, L, R, Z, FAR, ZL, ZR, ZF = range(8)
-HOP2 = {
-    "a": ((L, "xp", FAR), (Z, "xp", ZL), (Z, "xm", ZR)),
-    "b": ((R, "xm", FAR), (Z, "xm", ZR), (Z, "xp", ZL)),
-    "c": ((L, "xp", FAR), (Z, "xm", ZR), (L, "z", ZL)),
-    "d": ((R, "xm", FAR), (Z, "xp", ZL), (R, "z", ZR)),
-}
-HOP1 = ((O, "xp", L), (O, "xm", R), (O, "z", Z))
+
+
+def split(rows):
+    units = rows // 16
+    return 16 * round(units * 5 / 6)
+
+
+def copies(stage):
+    rows = SIZES[stage]
+    half, part = rows // 2, split(rows)
+    return [
+        (O, 0, rows, "xp", L),
+        (O, 0, rows, "xm", R),
+        (O, 0, rows, "z", Z),
+        (L, 0, half, "xp", FAR),
+        (R, half, rows, "xm", FAR),
+        (Z, 0, part, "xp", ZL),
+        (Z, 0, part, "xm", ZR),
+        (L, part, rows, "z", ZL),
+        (R, part, rows, "z", ZR),
+        (FAR, 0, rows, "z", ZF),
+    ]
+
+
+HOP1, FROM_L, FROM_R, FROM_Z, HOP3 = (0, 1, 2), (3, 7), (4, 8), (5, 6), (9,)
+TO_FAR, TO_ZLR = (3, 4), (5, 6, 7, 8)
 
 
 def column(slot, sibling=0):
@@ -84,30 +105,31 @@
 
     pl.semaphore_wait(barrier, 22)
 
-    def piece(stage, slot):
-        first, rows, _ = STAGES[stage]
-        return w.at[pl.ds(first, rows), pl.ds(column(slot), COLS)]
-
-    sent = []
-
-    def send(stage, src, to, dst):
-        cp = pltpu.make_async_remote_copy(
-            src_ref=piece(stage, src), dst_ref=piece(stage, dst),
-            send_sem=ss_w.at[stage, dst], recv_sem=rs_w.at[stage, dst],
+    def remote(stage, i):
+        src, low, high, to, dst = copies(stage)[i]
+        rows = pl.ds(STAGES[stage][0] + low, high - low)
+        return pltpu.make_async_remote_copy(
+            src_ref=w.at[rows, pl.ds(column(src), COLS)], dst_ref=w.at[rows, pl.ds(column(dst), COLS)],
+            send_sem=ss_w.at[stage, i], recv_sem=rs_w.at[stage, i],
             device_id=dev[to], device_id_type=MESH,
         )
-        cp.start()
-        sent.append(cp)
-
-    def arrive(stage, slot):
-        pltpu.make_async_remote_copy(
-            src_ref=piece(stage, slot), dst_ref=piece(stage, slot),
-            send_sem=ss_w.at[stage, slot], recv_sem=rs_w.at[stage, slot],
-            device_id=dev["z"], device_id_type=MESH,
-        ).wait_recv()
+
+    def send(stage, which):
+        for i in which:
+            remote(stage, i).start()
+
+    def arrive(stage, which):
+        for i in which:
+            remote(stage, i).wait_recv()
+
+    def sent(stage):
+        for i in range(10):
+            remote(stage, i).wait_send()
+        for group in range(2):
+            share_copy(stage, group).wait_send()
 
     def share_copy(stage, group):
-        first, rows, _ = STAGES[stage]
+        first, rows = STAGES[stage]
         return pltpu.make_async_remote_copy(
             src_ref=w.at[pl.ds(first, rows), pl.ds(group * 2048, 1024)],
             dst_ref=w.at[pl.ds(first, rows), pl.ds(group * 2048 + 1024, 1024)],
@@ -116,16 +138,10 @@
         )
 
     def share(stage, group):
-        cp = share_copy(stage, group)
-        cp.start()
-        sent.append(cp)
+        share_copy(stage, group).start()
 
     def shared(stage, group):
         share_copy(stage, group).wait_recv()
-
-    def hop1(stage):
-        for src, to, dst in HOP1:
-            send(stage, src, to, dst)
 
     row8 = lax.broadcasted_iota(jnp.int32, (8, 64), 0)
     col8 = lax.broadcasted_iota(jnp.int32, (8, 64), 1)
@@ -137,16 +153,27 @@
     by_a_t = (row64 // 8 == col64).astype(F32)
     dot = functools.partial(jnp.dot, precision=HIGH, preferred_element_type=F32)
 
-    q_sent, y_sent, z_sent = [], [], []
+    def query_copy(i, owner):
+        return pltpu.make_async_remote_copy(
+            src_ref=q_hbm, dst_ref=qbuf.at[owner], send_sem=ss_q.at[i], recv_sem=rs_q.at[owner],
+            device_id=((dp + i) % 16, tn), device_id_type=MESH,
+        )
+
+    def y_copy(i, owner):
+        return pltpu.make_async_remote_copy(
+            src_ref=ybuf.at[owner], dst_ref=ybuf.at[owner], send_sem=ss_y.at[i], recv_sem=rs_y.at[owner],
+            device_id=(dp, zh * 4 + (y + i) % 4), device_id_type=MESH,
+        )
+
+    def z_copy(owner):
+        return pltpu.make_async_remote_copy(
+            src_ref=zbuf.at[owner], dst_ref=zbuf.at[owner], send_sem=ss_z, recv_sem=rs_z,
+            device_id=(dp, (1 - zh) * 4 + y), device_id_type=MESH,
+        )
 
     def send_queries():
         for i in range(1, 16):
-            cp = pltpu.make_async_remote_copy(
-                src_ref=q_hbm, dst_ref=qbuf.at[dp], send_sem=ss_q.at[i], recv_sem=rs_q.at[dp],
-                device_id=((dp + i) % 16, tn), device_id_type=MESH,
-            )
-            cp.start()
-            q_sent.append(cp)
+            query_copy(i, dp).start()
 
     def input_part():
         load_li.wait()
@@ -154,34 +181,16 @@
         sign = (2 * sin[...] - 1).astype(F32).astype(BF16)
         ybuf[y] = lax.dot_general(sign, li[...], NT, preferred_element_type=F32) * D ** (-0.5)
         for i in range(1, 4):
-            cp = pltpu.make_async_remote_copy(
-                src_ref=ybuf.at[y], dst_ref=ybuf.at[y], send_sem=ss_y.at[i], recv_sem=rs_y.at[y],
-                device_id=(dp, zh * 4 + (y + i) % 4), device_id_type=MESH,
-            )
-            cp.start()
-            y_sent.append(cp)
+            y_copy(i, y).start()
 
     def input_sum():
         for i in range(1, 4):
-            other = (y + i) % 4
-            pltpu.make_async_remote_copy(
-                src_ref=ybuf.at[other], dst_ref=ybuf.at[other], send_sem=ss_y.at[i], recv_sem=rs_y.at[other],
-                device_id=(dp, tn), device_id_type=MESH,
-            ).wait_recv()
+            y_copy(i, (y + i) % 4).wait_recv()
         zbuf[zh] = ybuf[0] + ybuf[1] + ybuf[2] + ybuf[3]
-        cp = pltpu.make_async_remote_copy(
-            src_ref=zbuf.at[zh], dst_ref=zbuf.at[zh], send_sem=ss_z, recv_sem=rs_z,
-            device_id=(dp, (1 - zh) * 4 + y), device_id_type=MESH,
-        )
-        cp.start()
-        z_sent.append(cp)
+        z_copy(zh).start()
 
     def input_weigh():
-        other = 1 - zh
-        pltpu.make_async_remote_copy(
-            src_ref=zbuf.at[other], dst_ref=zbuf.at[other], send_sem=ss_z, recv_sem=rs_z,
-            device_id=(dp, other * 4 + y), device_id_type=MESH,
-        ).wait_recv()
+        z_copy(1 - zh).wait_recv()
         full = zbuf[0] + zbuf[1]
         pos = lax.broadcasted_iota(jnp.int32, (8, SLOTS), 1)
         for e in range(TOK // SLOTS):
@@ -201,11 +210,7 @@
             cp.wait()
         load_q.wait()
         for i in range(1, 16):
-            other = (dp + i) % 16
-            pltpu.make_async_remote_copy(
-                src_ref=q_hbm, dst_ref=qbuf.at[other], send_sem=ss_q.at[i], recv_sem=rs_q.at[other],
-                device_id=(dp, tn), device_id_type=MESH,
-            ).wait_recv()
+            query_copy(i, (dp + i) % 16).wait_recv()
         for i in range(16):
             qfull[pl.ds(4 * i, 4), :] = qbuf[i]
         kron = dot(dot(by_a_t, bi[...]), by_a) * dot(dot(by_b_t, bo[...]), by_b)
@@ -214,74 +219,99 @@
         mat[...] = jnp.zeros_like(mat)
         mat[pl.ds(0, 64), :] = dot(both, qfull[...])
 
-    def finish(j, product):
-        cols = pl.ds(j * BLOCK, BLOCK)
-        g = gate[:, cols].astype(F32)
+    def first_half(j):
+        rows = pl.ds(pl.multiple_of(j * BLOCK, BLOCK), BLOCK)
+        hid[j % 4] = lax.dot_general(
+            ct[:, pl.ds(0, 2048)], w[rows, pl.ds(0, 2048)], NT, preferred_element_type=F32
+        )
+
+    def second_half(j):
+        rows = pl.ds(pl.multiple_of(j * BLOCK, BLOCK), BLOCK)
+        product = hid[j % 4] + lax.dot_general(
+            ct[:, pl.ds(2048, 2048)], w[rows, pl.ds(2048, 2048)], NT, preferred_element_type=F32
+        )
+        g = gate[:, rows].astype(F32)
         up = (product * (g * (0.5 + 0.5 * jnp.tanh(0.5 * g)))).astype(BF16)
-        part = lax.dot_general(up, s64[:, cols], NT, preferred_element_type=F32)
-        if j == 0:
-            out64[...] = part
-        else:
-            out64[...] += part
-
-    def block(j):
-        if j == 0:
+        out64[...] += lax.dot_general(up, s64[:, rows], NT, preferred_element_type=F32)
+
+    def step_a(k):
+        if k + 1 < N:
+            send(k + 1, HOP1)
+        if k < N:
+            arrive(k, (0,))
+            send(k, FROM_L)
+            arrive(k, (1,))
+            send(k, FROM_R)
+            arrive(k, (2,))
+            send(k, FROM_Z)
+            share(k, 0)
+        if k == N - 1:
+            for s in (k - 1, k):
+                arrive(s, TO_FAR)
+                send(s, HOP3)
+        if k == 0:
+            send_queries()
+        if k == 1:
             for cp in load_c:
                 cp.wait()
-            load_gate.wait()
-        shared(j, 0)
-        shared(j, 1)
-        finish(j, lax.dot_general(ct[...], w[pl.ds(j * BLOCK, BLOCK), :], NT, preferred_element_type=F32))
-
-    last = HID // BLOCK - 1
-    last_rows = pl.ds(last * BLOCK, BLOCK)
-
-    own[0].wait()
-    hop1(0)
-    hop1(1)
-    own[1].wait()
-    for k in range(N + 3):
-        if k > 0 and k + 1 < N:
-            hop1(k + 1)
-        if k < N:
-            for slot in (L, R, Z):
-                arrive(k, slot)
-            for src, to, dst in HOP2[STAGES[k][2]]:
-                send(k, src, to, dst)
-            share(k, 0)
-        if 0 <= k - 1 < N:
-            for slot in (FAR, ZL, ZR):
-                arrive(k - 1, slot)
-            send(k - 1, FAR, "z", ZF)
-        if 0 <= k - 2 < N:
-            arrive(k - 2, ZF)
-            share(k - 2, 1)
+        if 1 <= k <= LAST:
+            shared(k - 1, 0)
+        if k == N - 1:
+            for s in IN_LAST:
+                shared(s, 0)
+
+    def step_b(k):
         if k == 0:
-            send_queries()
             input_part()
             hidden_signs()
+        if 1 <= k < N - 1:
+            arrive(k - 1, TO_FAR)
+            send(k - 1, HOP3)
         if k == 1:
             input_sum()
         if k == 2:
             input_weigh()
+            load_gate.wait()
+        if 3 <= k < N:
+            shared(k - 3, 1)
+        if k == N:
+            for s in IN_LAST:
+                shared(s, 1)
+
+    def step_c(k):
+        if 1 <= k < N:
+            arrive(k - 1, TO_ZLR)
+        if 2 <= k < N:
+            arrive(k - 2, (9,))
+            share(k - 2, 1)
+        if k == N - 1:
+            arrive(k, TO_ZLR)
+            for s in (k - 1, k):
+                arrive(s, (9,))
+                share(s, 1)
+        if k == 4:
             query_matrix()
-        if 0 <= k - 3 < last:
-            block(k - 3)
-        if k == N:
-            for s in range(last, N):
-                shared(s, 0)
-            hid[...] = lax.dot_general(
-                ct[:, pl.ds(0, 2048)], w[last_rows, pl.ds(0, 2048)], NT, preferred_element_type=F32
-            )
-    for s in range(last, N):
-        shared(s, 1)
-    finish(
-        last,
-        hid[...]
-        + lax.dot_general(
-            ct[:, pl.ds(2048, 2048)], w[last_rows, pl.ds(2048, 2048)], NT, preferred_element_type=F32
-        ),
-    )
+        if 4 <= k < N:
+            sent(k - 4)
+
+    def step(k, _):
+        def only(part):
+            for i in range(N + 1):
+                pl.when(k == i)(functools.partial(part, i))
+
+        only(step_a)
+        first = jnp.where(k == N - 1, LAST, jnp.where(k <= LAST, k - 1, -1))
+        pl.when(first >= 0)(lambda: first_half(first))
+        only(step_b)
+        pl.when(k >= 3)(lambda: second_half(k - 3))
+        only(step_c)
+        return 0
+
+    out64[...] = jnp.zeros_like(out64)
+    own[0].wait()
+    send(0, HOP1)
+    own[1].wait()
+    lax.fori_loop(0, N + 1, step, 0)
 
     rows = [
         jnp.sum(in64[pl.ds(e * SLOTS, SLOTS), :] * out64[pl.ds(e * SLOTS, SLOTS), :], axis=0, keepdims=True)
@@ -298,8 +328,13 @@
         )
         cp.start()
         g_sent.append(cp)
-    for cp in sent + q_sent + y_sent + z_sent:
-        cp.wait_send()
+    for s in range(N - 4, N):
+        sent(s)
+    for i in range(1, 16):
+        query_copy(i, dp).wait_send()
+    for i in range(1, 4):
+        y_copy(i, y).wait_send()
+    z_copy(zh).wait_send()
     for i in range(1, 8):
         other = (tn + i) % 8
         pltpu.make_async_remote_copy(
@@ -345,9 +380,9 @@
             vmem((8, 8, 128), F32),
             vmem((TOK, 64), F32),
             vmem((64, HID), BF16),
-            vmem((TOK, BLOCK), F32),
+            vmem((4, TOK, BLOCK), F32),
             vmem((TOK, 64), F32),
-            dma((N, 8)), dma((N, 8)), dma((N, 2)), dma((N, 2)), dma((16,)), dma((16,)),
+            dma((N, 10)), dma((N, 10)), dma((N, 2)), dma((N, 2)), dma((16,)), dma((16,)),
             dma((4,)), dma((4,)), dma, dma, dma((8,)), dma((8,)), dma((32,)),
         ],
         compiler_params=pltpu.CompilerParams(

time: 86.4 us -> 76.6 us (0.89)
  Pallas kernels: 83.5 us -> 74.1 us
    pallas_call x1, Pallas kernels: 83.5 us -> 74.1 us  [on_device(): pl.pallas_call(kernel, out_shape=jax.ShapeDtypeStruct((4, 512), F32), in_...]
where the time goes in v2:
time: 76.6 us; the launch traced here: 75.4 us
  Pallas kernels  74.1 us (97%)
  local copies, waits for them, and re-layouts  1.3 us (2%)
    pallas_call x1, Pallas kernels, on_device(): pl.pallas_call(kernel, out_shape=jax.ShapeDtypeStruct((4, 512), F32), in_...  74.1 us

profile of v2, /device:TPU:0, one launch (start us, length us, event | category | flops | bytes accessed | tf_op | source)
XLA Modules:
  0.0 75.4 jit_solution(13673630213774241252)
XLA Ops:
  0.0 74.1 %scores.1 = f32[4,512]{1,0:T(4,128)} custom-call(bf16[1024,512]{1,0:T(8,128)(2,1)} %bitcast.8, bf16[1024,4096]{1,0:T(8,128)(2,1)} %bitcast.6, bf16[1024,1792]{1,0:T(8,128)(2,1)} %bitcast.7, bf16[1792,256]{1,0:T(8,128)(2,1)} %w_hbm.1, s32[4]{0:T(128)} %len_ref.1, s32[8,512]{1,0:T(8,128)} %bitcast.10, s32[8,1792]{1,0:T(8,128)} %bitcast.9, f32[8,8]{1,0:T(8,128)} %bi_hbm.1, ...), custom_call_target="tpu_custom_call" | custom-call | flops 15032385536 | bytes 30000000 | tf_op jit(solution)/shard_map/scores/pallas_call | solution.py:360
  74.1 1.3 %copy.13 = f32[4,512]{1,0:T(4,128)} copy(f32[4,512]{1,0:T(4,128)} %scores.1) | data formatting | bytes 16384

commit v3 on v2

v3 whole, which is shorter than its diff:
```python
import functools

import jax
import jax.numpy as jnp
from jax import lax
from jax.experimental import pallas as pl
from jax.experimental.pallas import tpu as pltpu
from jax.sharding import PartitionSpec as P

MESH = pl.DeviceIdType.MESH
HIGH = lax.Precision.HIGHEST
F32, BF16 = jnp.float32, jnp.bfloat16
D, FF, RA, RG = 4096, 14336, 8, 8
SHIFT = 0.1
TOK, HID, COLS, SLOTS = 1024, 1792, 256, 256
BLOCK = 256
NT = (((1,), (1,)), ((), ()))

N = HID // BLOCK
ALONG_X = (14, 13, 13, 13, 14, 14, 13)
SCHEDULE = (
    (
        (
            (0, 0, 0), (0, 0, 1), (0, 0, 2), (0, 1, 0), (0, 1, 1), (0, 1, 2), (2, 1, 0), (2, 0, 0),
            (0, 2, 0), (0, 2, 1), (0, 2, 2), (0, 0, 3), (0, 0, 4), (0, 0, 9), (0, 0, 8), (0, 3, 2),
            (0, 3, 0), (0, 3, 1), (2, 2, 0), (0, 1, 9), (0, 1, 8), (0, 1, 3), (0, 1, 4), (0, 4, 2),
            (0, 2, 3), (0, 2, 4), (1, 0, 0), (2, 4, 0), (0, 4, 0), (0, 4, 1), (0, 0, 7),
        ),
        (0, 0),
    ),
    (
        (
            (0, 3, 3), (0, 3, 4), (0, 1, 7), (1, 1, 0), (2, 3, 0), (0, 0, 5), (0, 0, 6), (1, 2, 0),
            (0, 2, 7),
        ),
        (0, 1),
    ),
    (
        (
            (0, 4, 3), (0, 5, 0), (0, 4, 4), (0, 5, 1), (1, 0, 2),
        ),
        (0, 2),
    ),
    (
        (
            (0, 3, 7), (1, 3, 0), (0, 1, 5), (0, 1, 6), (1, 1, 2), (0, 2, 8), (1, 0, 1), (0, 2, 9),
        ),
        (0, 3),
    ),
    (
        (
            (0, 6, 0), (0, 6, 1), (0, 4, 7), (1, 2, 2), (1, 4, 0),
        ),
        (1, 0),
    ),
    (
        (
            (0, 5, 3), (0, 5, 4), (0, 5, 2), (1, 3, 2),
        ),
        (0, 4),
    ),
    (
        (
            (0, 2, 5), (0, 2, 6), (0, 3, 9), (0, 3, 8), (1, 1, 1), (0, 6, 2), (0, 3, 5), (0, 3, 6),
            (1, 4, 2),
        ),
        (1, 1),
    ),
    (
        (
            (0, 6, 3), (0, 6, 4), (0, 5, 7), (0, 4, 5), (0, 4, 6), (1, 5, 0), (1, 2, 1), (0, 4, 9),
            (0, 4, 8), (0, 5, 9), (0, 5, 5), (0, 5, 6), (0, 5, 8),
        ),
        (0, 5),
    ),
    (
        (
            (0, 6, 8), (0, 6, 9), (1, 3, 1),
        ),
        (1, 2),
    ),
    (
        (
            (0, 6, 5), (0, 6, 6), (0, 6, 7), (1, 6, 0),
        ),
        (1, 3),
    ),
    (
        (
            (1, 4, 1), (1, 5, 2),
        ),
        (0, 6),
    ),
    (
        (
            (1, 5, 1),
        ),
        (1, 4),
    ),
    (
        (
            (1, 6, 2), (1, 6, 1),
        ),
        (1, 5),
    ),
    (
        (
        ),
        (1, 6),
    ),
)
O, L, R, Z, FAR, ZL, ZR, ZF = range(8)


FAR_FIRST = (2, 1, 3, 0)


def copies(stage):
    rows, half = BLOCK, BLOCK // 2
    part = 16 * ALONG_X[stage]
    return [
        (O, 0, rows, "xp", L),
        (O, 0, rows, "xm", R),
        (O, 0, rows, "z", Z),
        (L, 0, half, "xp", FAR),
        (R, half, rows, "xm", FAR),
        (Z, 0, part, "xp", ZL),
        (Z, 0, part, "xm", ZR),
        (FAR, 0, rows, "z", ZF),
    ] + [(L, part, rows, "z", ZL), (R, part, rows, "z", ZR)] * (part < rows)


AFTER = ((), (), (), (0,), (1,), (2,), (2,), (3, 4), (0,), (1,))
GROUPS = ((0, 1280), (2560, 512), (3072, 256))
BROUGHT = ((0, 1, 2, 3, 4), (5, 6, 8, 9), (7,))


def plan():
    arrived, steps = set(), []
    for actions, _ in SCHEDULE:
        steps.append([])
        for what, at, which in actions:
            needed = ((AFTER, BROUGHT, ((),))[what])[which]
            new = [i for i in needed if i < len(copies(at)) and (at, i) not in arrived]
            arrived.update((at, i) for i in new)
            steps[-1].append((new, (what, at, which)))
    return steps


PLAN = plan()


def column(slot):
    return slot * COLS if slot < 5 else 2560 + (slot - 5) * COLS


def sibling_column(col):
    return col + (1280 if col < 1280 else 768)


def kernel(
    li_hbm, ct_hbm, gate_hbm, w_hbm, len_ref, sin_hbm, shid_hbm, bi_hbm, bo_hbm, ev_hbm, q_hbm,
    o_ref,
    w, ct, gate, li, sin, shid, bi, bo, ev, qbuf, qfull, mat, ybuf, zbuf, gbuf, in64, s64, hid, act, out64,
    ss_w, rs_w, ss_s, rs_s, ss_q, rs_q, ss_y, rs_y, ss_z, rs_z, ss_g, rs_g, lsem,
):
    dp, tn = lax.axis_index("dp"), lax.axis_index("tensor")
    x, z, c = dp // 4, (dp // 2) % 2, dp % 2
    zh, y = tn // 4, tn % 4
    xp, xm = (x + 1) % 4, (x + 3) % 4
    at = lambda xx, zz, cc: xx * 4 + zz * 2 + cc
    dev = {
        "xp": (at(xp, z, c), tn),
        "xm": (at(xm, z, c), tn),
        "z": (at(x, 1 - z, c), tn),
        "sib": (at(x, z, 1 - c), tn),
    }

    loads = []

    def load(src, dst):
        cp = pltpu.make_async_copy(src, dst, lsem.at[len(loads)])
        loads.append(cp)
        cp.start()
        return cp

    own = load(w_hbm, w.at[:, pl.ds(0, COLS)])

    barrier = pltpu.get_barrier_semaphore()
    for i in range(1, 16):
        pl.semaphore_signal(barrier, inc=1, device_id=((dp + i) % 16, tn), device_id_type=MESH)
    for i in range(1, 8):
        pl.semaphore_signal(barrier, inc=1, device_id=(dp, (tn + i) % 8), device_id_type=MESH)

    load_li = load(li_hbm, li)
    load_sin = load(sin_hbm, sin)
    load_q = load(q_hbm, qbuf.at[dp])
    load_small = [load(bi_hbm, bi), load(bo_hbm, bo), load(ev_hbm, ev), load(shid_hbm, shid)]
    load_c = []
    for half in range(2):
        cc = c if half == 0 else 1 - c
        for slot, (xx, zz) in enumerate(
            ((x, z), (xm, z), (xp, z), (x, 1 - z), ((x + 2) % 4, z), (xm, 1 - z), (xp, 1 - z), ((x + 2) % 4, 1 - z))
        ):
            first = pl.multiple_of(at(xx, zz, cc) * COLS, COLS)
            load_c.append(load(ct_hbm.at[:, pl.ds(first, COLS)], ct.at[:, pl.ds(sibling_column(column(slot)) if half else column(slot), COLS)]))
    load_gate = load(gate_hbm, gate)

    pl.semaphore_wait(barrier, 22)

    def remote(stage, i):
        src, low, high, to, dst = copies(stage)[i]
        rows = pl.ds(stage * BLOCK + low, high - low)
        return pltpu.make_async_remote_copy(
            src_ref=w.at[rows, pl.ds(column(src), COLS)], dst_ref=w.at[rows, pl.ds(column(dst), COLS)],
            send_sem=ss_w.at[stage, i], recv_sem=rs_w.at[stage, i],
            device_id=dev[to], device_id_type=MESH,
        )

    def share_copy(stage, group):
        rows = pl.ds(stage * BLOCK, BLOCK)
        col, cols = GROUPS[group]
        return pltpu.make_async_remote_copy(
            src_ref=w.at[rows, pl.ds(col, cols)], dst_ref=w.at[rows, pl.ds(sibling_column(col), cols)],
            send_sem=ss_s.at[stage, group], recv_sem=rs_s.at[stage, group],
            device_id=dev["sib"], device_id_type=MESH,
        )

    def shared(stage, group):
        share_copy(stage, group).wait_recv()

    def sent(stage):
        for i in range(len(copies(stage))):
            remote(stage, i).wait_send()
        for group in range(3):
            share_copy(stage, group).wait_send()

    row8 = lax.broadcasted_iota(jnp.int32, (8, 128), 0)
    col8 = lax.broadcasted_iota(jnp.int32, (8, 128), 1)
    by_b = (col8 % 8 == row8).astype(F32)
    by_a = (col8 % 64 // 8 == row8).astype(F32)
    row_t = lax.broadcasted_iota(jnp.int32, (128, 8), 0)
    col_t = lax.broadcasted_iota(jnp.int32, (128, 8), 1)
    by_b_t = (row_t % 8 == col_t).astype(F32)
    by_a_t = (row_t % 64 // 8 == col_t).astype(F32)
    dot = functools.partial(jnp.dot, precision=HIGH, preferred_element_type=F32)

    def query_copy(i, owner):
        return pltpu.make_async_remote_copy(
            src_ref=q_hbm, dst_ref=qbuf.at[owner], send_sem=ss_q.at[i], recv_sem=rs_q.at[owner],
            device_id=((dp + i) % 16, tn), device_id_type=MESH,
        )

    def y_copy(i, owner):
        return pltpu.make_async_remote_copy(
            src_ref=ybuf.at[owner], dst_ref=ybuf.at[owner], send_sem=ss_y.at[i], recv_sem=rs_y.at[owner],
            device_id=(dp, zh * 4 + (y + i) % 4), device_id_type=MESH,
        )

    def z_copy(owner):
        return pltpu.make_async_remote_copy(
            src_ref=zbuf.at[owner], dst_ref=zbuf.at[owner], send_sem=ss_z, recv_sem=rs_z,
            device_id=(dp, (1 - zh) * 4 + y), device_id_type=MESH,
        )

    def send_queries():
        for i in range(1, 16):
            query_copy(i, dp).start()

    def input_part():
        load_li.wait()
        load_sin.wait()
        sign = (2 * sin[...] - 1).astype(F32).astype(BF16)
        ybuf[y] = lax.dot_general(sign, li[...], NT, preferred_element_type=F32) * D ** (-0.5)
        for i in range(1, 4):
            y_copy(i, y).start()

    def input_sum():
        for i in range(1, 4):
            y_copy(i, (y + i) % 4).wait_recv()
        zbuf[zh] = ybuf[0] + ybuf[1] + ybuf[2] + ybuf[3]
        z_copy(zh).start()

    def input_weigh():
        z_copy(1 - zh).wait_recv()
        full = zbuf[0] + zbuf[1]
        pos = lax.broadcasted_iota(jnp.int32, (8, SLOTS), 1)
        for e in range(TOK // SLOTS):
            count = len_ref[e]
            scale = FF ** (-0.5) / count.astype(F32)
            part = full[:, e * SLOTS : (e + 1) * SLOTS]
            part = jnp.where(pos < count, part * scale, 0.0)
            in64[pl.ds(e * SLOTS, SLOTS), :] = dot(part.T, by_a)

    def hidden_signs():
        load_small[3].wait()
        sign = (2 * shid[...] - 1).astype(F32)
        s64[...] = jnp.dot(by_b_t.astype(BF16), sign.astype(BF16), preferred_element_type=F32).astype(BF16)

    def query_matrix():
        for cp in load_small[:3]:
            cp.wait()
        load_q.wait()
        for i in range(1, 16):
            query_copy(i, (dp + i) % 16).wait_recv()
        for i in range(16):
            qfull[pl.ds(4 * i, 4), :] = qbuf[i]
        kron = dot(dot(by_a_t, bi[...]), by_a[:, :64]) * dot(dot(by_b_t, bo[...]), by_b[:, :64])
        values = jnp.sum(dot(ev[...], by_b[:, :64]) * by_a[:, :64], axis=0, keepdims=True)
        both = lax.dot_general(kron / (values + SHIFT), kron[:64], NT, precision=HIGH, preferred_element_type=F32)
        twice = dot(both, qfull[...])
        top = twice.astype(BF16)
        rest = (twice - top.astype(F32)).astype(BF16)
        both_parts = jnp.concatenate([top[:64], rest[:64]], axis=0)
        mat[pl.ds(0, 128), :] = both_parts
        mat[pl.ds(128, 128), :] = both_parts

    def first_part(j):
        rows = pl.ds(pl.multiple_of(j * BLOCK, BLOCK), BLOCK)
        hid[j % 4] = lax.dot_general(
            ct[:, pl.ds(0, 2560)], w[rows, pl.ds(0, 2560)], NT, preferred_element_type=F32
        )
        g = gate[:, rows].astype(F32)
        act[j % 4] = g * (0.5 + 0.5 * jnp.tanh(0.5 * g))

    def second_part(j):
        rows = pl.ds(pl.multiple_of(j * BLOCK, BLOCK), BLOCK)
        product = hid[j % 4] + lax.dot_general(
            ct[:, pl.ds(2560, 1536)], w[rows, pl.ds(2560, 1536)], NT, preferred_element_type=F32
        )
        up = (product * act[j % 4]).astype(BF16)
        out64[...] += lax.dot_general(up, s64[:, rows], NT, preferred_element_type=F32)

    def step_actions(i):
        part, j = SCHEDULE[i][1]
        for arrivals, (what, at, which) in PLAN[i]:
            for copy in arrivals:
                remote(at, copy).wait_recv()
            if what == 0:
                remote(at, which).start()
            elif what == 1:
                share_copy(at, which).start()
            else:
                small[at]()
        if i == len(SCHEDULE) - 1:
            for stage in range(5):
                sent(stage)
        if part == 0 and j == 0:
            for cp in load_c:
                cp.wait()
            load_gate.wait()
        for group in ((0,), (1, 2))[part]:
            shared(j, group)

    def block_of(step, part):
        j = jnp.int32(-1)
        for i, (_, (which, block)) in enumerate(SCHEDULE):
            if which == part:
                j = jnp.where(step == i, block, j)
        return j

    def step(k, _):
        for i in range(len(SCHEDULE)):
            pl.when(k == i)(functools.partial(step_actions, i))
        first, second = block_of(k, 0), block_of(k, 1)
        pl.when(first >= 0)(lambda: first_part(first))
        pl.when(second >= 0)(lambda: second_part(second))
        return 0

    def input_start():
        send_queries()
        input_part()

    small = (input_start, hidden_signs, input_sum, input_weigh, query_matrix)
    out64[...] = jnp.zeros_like(out64)
    own.wait()
    lax.fori_loop(0, len(SCHEDULE), step, 0)

    rows = [
        jnp.sum(in64[pl.ds(e * SLOTS, SLOTS), :] * out64[pl.ds(e * SLOTS, SLOTS), :], axis=0, keepdims=True)
        for e in range(TOK // SLOTS)
    ]
    gbuf[tn] = jnp.zeros((8, 128), F32)
    for e in range(TOK // SLOTS):
        gbuf[tn, pl.ds(e, 1), :] = rows[e]

    def g_copy(i, owner):
        return pltpu.make_async_remote_copy(
            src_ref=gbuf.at[owner], dst_ref=gbuf.at[owner], send_sem=ss_g.at[i], recv_sem=rs_g.at[owner],
            device_id=(dp, (zh + 1 - i // 4) % 2 * 4 + (y + FAR_FIRST[i % 4]) % 4), device_id_type=MESH,
        )

    for i in range(7):
        g_copy(i, tn).start()
    for stage in range(5, N):
        sent(stage)
    for i in range(1, 16):
        query_copy(i, dp).wait_send()
    for i in range(1, 4):
        y_copy(i, y).wait_send()
    z_copy(zh).wait_send()
    for i in range(1, 8):
        g_copy(0, (tn + i) % 8).wait_recv()
    total = gbuf[0]
    for i in range(1, 8):
        total = total + gbuf[i]
    top = total.astype(BF16)
    rest = (total - top.astype(F32)).astype(BF16)
    both = jnp.concatenate([top, rest], axis=1)
    o_ref[...] = jnp.dot(both, mat[...], preferred_element_type=F32)[:4, :]
    for i in range(7):
        g_copy(i, tn).wait_send()


def on_device(
    layer_input, output_cotangent, gate_preact, down_weight, lengths, input_signs, hidden_signs,
    basis_in, basis_out, eigenvalues, query_grads,
):
    any_spec = pl.BlockSpec(memory_space=pl.ANY)
    vmem, dma = pltpu.VMEM, pltpu.SemaphoreType.DMA
    specs = [any_spec] * 11
    specs[4] = pl.BlockSpec(memory_space=pltpu.SMEM)
    return pl.pallas_call(
        kernel,
        out_shape=jax.ShapeDtypeStruct((4, 512), F32),
        in_specs=specs,
        out_specs=pl.BlockSpec(memory_space=pltpu.VMEM),
        scratch_shapes=[
            vmem((HID, D), BF16),
            vmem((TOK, D), BF16),
            vmem((TOK, HID), BF16),
            vmem((TOK, 512), BF16),
            vmem((8, 512), jnp.int32),
            vmem((8, HID), jnp.int32),
            vmem((8, 8), F32),
            vmem((8, 8), F32),
            vmem((8, 8), F32),
            vmem((16, 4, 512), F32),
            vmem((64, 512), F32),
            vmem((256, 512), BF16),
            vmem((4, 8, TOK), F32),
            vmem((2, 8, TOK), F32),
            vmem((8, 8, 128), F32),
            vmem((TOK, 128), F32),
            vmem((128, HID), BF16),
            vmem((4, TOK, BLOCK), F32),
            vmem((4, TOK, BLOCK), F32),
            vmem((TOK, 128), F32),
            dma((N, 10)), dma((N, 10)), dma((N, 3)), dma((N, 3)), dma((16,)), dma((16,)),
            dma((4,)), dma((4,)), dma, dma, dma((8,)), dma((8,)), dma((32,)),
        ],
        compiler_params=pltpu.CompilerParams(
            collective_id=0, has_side_effects=True, vmem_limit_bytes=56 * 1024 * 1024
        ),
        cost_estimate=pl.CostEstimate(flops=2 * TOK * HID * D, bytes_accessed=30_000_000, transcendentals=TOK * HID),
        name="scores",
    )(
        layer_input.reshape(TOK, 512),
        output_cotangent.reshape(TOK, D),
        gate_preact.reshape(TOK, HID),
        down_weight,
        lengths,
        input_signs.T,
        hidden_signs.T,
        basis_in,
        basis_out,
        eigenvalues,
        query_grads.T,
    )


def solution(mesh):
    in_specs = (
        P("dp", None, "tensor"),
        P("dp", None, None),
        P("dp", None, "tensor"),
        P("tensor", "dp"),
        P("dp"),
        P("tensor", None),
        P("tensor", None),
        P(),
        P(),
        P(),
        P("tensor", "dp"),
    )
    return jax.shard_map(
        on_device, mesh=mesh, in_specs=in_specs, out_specs=P("dp", "tensor"), check_vma=False
    )
```

time: 76.6 us -> 70.4 us (0.919); the launches traced: 75.4 us -> 70.2 us
  Pallas kernels: 74.1 us -> 68.9 us
    pallas_call x1, Pallas kernels: 74.1 us -> 68.9 us  [on_device(): pl.pallas_call(kernel, out_shape=jax.ShapeDtypeStruct((4, 512), F32), in_...]
where the time goes in v3:
time: 70.4 us; the launch traced here: 70.2 us
  Pallas kernels  68.9 us (98%)
  local copies, waits for them, and re-layouts  1.3 us (2%)
    pallas_call x1, Pallas kernels, on_device(): pl.pallas_call(kernel, out_shape=jax.ShapeDtypeStruct((4, 512), F32), in_...  68.9 us

profile of v3, /device:TPU:0, one launch (start us, length us, event | category | flops | bytes accessed | tf_op | source)
XLA Modules:
  0.0 70.2 jit_solution(12015000593351010457)
XLA Ops:
  0.0 68.9 %scores.1 = f32[4,512]{1,0:T(4,128)} custom-call(bf16[1024,512]{1,0:T(8,128)(2,1)} %bitcast.8, bf16[1024,4096]{1,0:T(8,128)(2,1)} %bitcast.6, bf16[1024,1792]{1,0:T(8,128)(2,1)} %bitcast.7, bf16[1792,256]{1,0:T(8,128)(2,1)} %w_hbm.1, s32[4]{0:T(128)} %len_ref.1, s32[8,512]{1,0:T(8,128)} %bitcast.10, s32[8,1792]{1,0:T(8,128)} %bitcast.9, f32[8,8]{1,0:T(8,128)} %bi_hbm.1, ...), custom_call_target="tpu_custom_call" | custom-call | flops 15032385536 | bytes 30000000 | tf_op jit(solution)/shard_map/scores/pallas_call | solution.py:423
  68.9 1.3 %copy.13 = f32[4,512]{1,0:T(4,128)} copy(f32[4,512]{1,0:T(4,128)} %scores.1) | data formatting | bytes 16384

commit v4 on v3

--- a/solution.py
+++ b/solution.py
@@ -17,132 +17,163 @@
 NT = (((1,), (1,)), ((), ()))
 
 N = HID // BLOCK
-ALONG_X = (14, 13, 13, 13, 14, 14, 13)
+PEER, GATES = N - 1, N
+ALONG_X = (16, 16, 16, 16, 16)
 SCHEDULE = (
     (
         (
-            (0, 0, 0), (0, 0, 1), (0, 0, 2), (0, 1, 0), (0, 1, 1), (0, 1, 2), (2, 1, 0), (2, 0, 0),
-            (0, 2, 0), (0, 2, 1), (0, 2, 2), (0, 0, 3), (0, 0, 4), (0, 0, 9), (0, 0, 8), (0, 3, 2),
-            (0, 3, 0), (0, 3, 1), (2, 2, 0), (0, 1, 9), (0, 1, 8), (0, 1, 3), (0, 1, 4), (0, 4, 2),
-            (0, 2, 3), (0, 2, 4), (1, 0, 0), (2, 4, 0), (0, 4, 0), (0, 4, 1), (0, 0, 7),
+            (0, 0, 0), (0, 0, 1), (0, 0, 2), (0, 6, 0), (0, 1, 0), (0, 1, 1), (0, 1, 2), (2, 0, 0),
+            (0, 2, 0), (0, 2, 1), (0, 2, 2), (0, 7, 0), (0, 6, 1), (2, 3, 0), (0, 0, 5), (0, 0, 6),
+            (0, 3, 2), (2, 1, 0), (2, 2, 0), (0, 7, 1), (0, 0, 3), (0, 0, 4), (0, 7, 4), (0, 7, 2),
+            (0, 1, 3), (0, 1, 4), (2, 4, 0), (2, 5, 0), (0, 2, 3), (0, 2, 4), (0, 4, 2), (0, 7, 3),
+            (0, 3, 0), (0, 3, 1), (1, 0, 1), (0, 7, 5), (1, 0, 0), (2, 6, 0), (0, 6, 2), (0, 4, 0),
+            (0, 4, 1), (1, 1, 0),
         ),
         (0, 0),
     ),
     (
         (
-            (0, 3, 3), (0, 3, 4), (0, 1, 7), (1, 1, 0), (2, 3, 0), (0, 0, 5), (0, 0, 6), (1, 2, 0),
-            (0, 2, 7),
+            (0, 0, 7), (0, 0, 8), (0, 7, 6), (1, 2, 0),
         ),
         (0, 1),
     ),
     (
         (
-            (0, 4, 3), (0, 5, 0), (0, 4, 4), (0, 5, 1), (1, 0, 2),
+            (0, 3, 3), (0, 3, 4), (0, 7, 7), (2, 7, 0), (0, 5, 0), (0, 5, 1), (0, 5, 2),
         ),
         (0, 2),
     ),
     (
         (
-            (0, 3, 7), (1, 3, 0), (0, 1, 5), (0, 1, 6), (1, 1, 2), (0, 2, 8), (1, 0, 1), (0, 2, 9),
+            (0, 4, 3), (0, 4, 4), (0, 6, 3), (1, 0, 2), (0, 1, 5), (0, 1, 6), (0, 1, 7), (1, 3, 0),
+        ),
+        (1, 0),
+    ),
+    (
+        (
         ),
         (0, 3),
     ),
     (
         (
-            (0, 6, 0), (0, 6, 1), (0, 4, 7), (1, 2, 2), (1, 4, 0),
-        ),
-        (1, 0),
-    ),
-    (
-        (
-            (0, 5, 3), (0, 5, 4), (0, 5, 2), (1, 3, 2),
+            (0, 5, 3), (0, 2, 5), (0, 5, 4), (0, 2, 6), (0, 2, 7), (1, 4, 0), (1, 6, 1), (1, 6, 2),
+            (0, 3, 7), (0, 3, 5), (0, 3, 6), (1, 1, 1), (1, 1, 2),
         ),
         (0, 4),
     ),
     (
         (
-            (0, 2, 5), (0, 2, 6), (0, 3, 9), (0, 3, 8), (1, 1, 1), (0, 6, 2), (0, 3, 5), (0, 3, 6),
-            (1, 4, 2),
+            (0, 4, 7), (1, 5, 0),
         ),
         (1, 1),
     ),
     (
         (
-            (0, 6, 3), (0, 6, 4), (0, 5, 7), (0, 4, 5), (0, 4, 6), (1, 5, 0), (1, 2, 1), (0, 4, 9),
-            (0, 4, 8), (0, 5, 9), (0, 5, 5), (0, 5, 6), (0, 5, 8),
+            (0, 4, 5), (0, 4, 6), (1, 2, 2), (1, 6, 0), (1, 2, 1), (0, 5, 7),
         ),
         (0, 5),
     ),
     (
         (
-            (0, 6, 8), (0, 6, 9), (1, 3, 1),
+            (0, 5, 5), (0, 5, 6), (1, 3, 2),
+        ),
+        (0, 6),
+    ),
+    (
+        (
+            (1, 3, 1),
+        ),
+        (1, 6),
+    ),
+    (
+        (
+            (1, 4, 2), (1, 4, 1),
         ),
         (1, 2),
     ),
     (
         (
-            (0, 6, 5), (0, 6, 6), (0, 6, 7), (1, 6, 0),
+            (1, 5, 2),
         ),
         (1, 3),
     ),
     (
         (
-            (1, 4, 1), (1, 5, 2),
-        ),
-        (0, 6),
-    ),
-    (
-        (
             (1, 5, 1),
         ),
         (1, 4),
     ),
     (
         (
-            (1, 6, 2), (1, 6, 1),
         ),
         (1, 5),
     ),
-    (
-        (
-        ),
-        (1, 6),
-    ),
 )
-O, L, R, Z, FAR, ZL, ZR, ZF = range(8)
-
-
+
+O, L, R, FAR, Z, ZL, ZR, ZF = range(8)
 FAR_FIRST = (2, 1, 3, 0)
 
 
 def copies(stage):
     rows, half = BLOCK, BLOCK // 2
-    part = 16 * ALONG_X[stage]
-    return [
-        (O, 0, rows, "xp", L),
-        (O, 0, rows, "xm", R),
-        (O, 0, rows, "z", Z),
-        (L, 0, half, "xp", FAR),
-        (R, half, rows, "xm", FAR),
+    hop1 = [(O, 0, rows, "xp", L), (O, 0, rows, "xm", R), (O, 0, rows, "z", Z)]
+    far = [(L, 0, half, "xp", FAR), (R, half, rows, "xm", FAR)]
+    if stage == 0:
+        return hop1 + far + [
+            (Z, 0, rows, "xp", ZL),
+            (Z, 0, rows, "xm", ZR),
+            (ZL, 0, half, "xp", ZF),
+            (ZR, half, rows, "xm", ZF),
+        ]
+    if stage == PEER:
+        return [(O, 0, rows, "cross", Z), (Z, 0, rows, "cross", O), (L, 0, rows, "cross", ZL), (ZL, 0, rows, "cross", L)]
+    if stage == GATES:
+        return [None] * 8
+    part = 16 * ALONG_X[stage - 1]
+    return hop1 + far + [
         (Z, 0, part, "xp", ZL),
         (Z, 0, part, "xm", ZR),
         (FAR, 0, rows, "z", ZF),
     ] + [(L, part, rows, "z", ZL), (R, part, rows, "z", ZR)] * (part < rows)
 
 
-AFTER = ((), (), (), (0,), (1,), (2,), (2,), (3, 4), (0,), (1,))
+def after(stage, i):
+    if stage == PEER:
+        return [(0, j) for j in ((), (2,), (0, 1, 3, 4), (5, 6, 7, 8))[i]]
+    if stage == GATES:
+        return [(GATES, i - 4)] if i >= 4 else []
+    if stage == 0:
+        return [(0, j) for j in ((), (), (), (0,), (1,), (2,), (2,), (5,), (6,))[i]]
+    return [(stage, j) for j in ((), (), (), (0,), (1,), (2,), (2,), (3, 4), (0,), (1,))[i]]
+
+
 GROUPS = ((0, 1280), (2560, 512), (3072, 256))
-BROUGHT = ((0, 1, 2, 3, 4), (5, 6, 8, 9), (7,))
+
+
+def brought(stage, group):
+    if stage == PEER:
+        which = ((0, 1, 3), (2,), (2,))[group]
+    elif stage == 0:
+        which = ((0, 1, 2, 3, 4), (5, 6), (7, 8))[group]
+    else:
+        which = ((0, 1, 2, 3, 4), (5, 6, 8, 9), (7,))[group]
+    return [(stage, i) for i in which if i < len(copies(stage))]
 
 
 def plan():
     arrived, steps = set(), []
-    for actions, _ in SCHEDULE:
+    for actions, (part, block) in SCHEDULE:
         steps.append([])
-        for what, at, which in actions:
-            needed = ((AFTER, BROUGHT, ((),))[what])[which]
-            new = [i for i in needed if i < len(copies(at)) and (at, i) not in arrived]
-            arrived.update((at, i) for i in new)
+        for what, at, which in actions + ((3, part, block),):
+            needed = ()
+            if what == 0:
+                needed = after(at, which)
+            elif what == 1:
+                needed = brought(at, which)
+            elif what == 3 and part == 0 and block == PEER:
+                needed = [(GATES, i) for i in range(4, 8)]
+            new = [x for x in needed if x not in arrived]
+            arrived.update(new)
             steps[-1].append((new, (what, at, which)))
     return steps
 
@@ -161,8 +192,8 @@
 def kernel(
     li_hbm, ct_hbm, gate_hbm, w_hbm, len_ref, sin_hbm, shid_hbm, bi_hbm, bo_hbm, ev_hbm, q_hbm,
     o_ref,
-    w, ct, gate, li, sin, shid, bi, bo, ev, qbuf, qfull, mat, ybuf, zbuf, gbuf, in64, s64, hid, act, out64,
-    ss_w, rs_w, ss_s, rs_s, ss_q, rs_q, ss_y, rs_y, ss_z, rs_z, ss_g, rs_g, lsem,
+    w, ct, gate, give_w, give_gate, relay, li, sin, shid, bi, bo, ev, qbuf, qfull, mat, ybuf, zbuf, gbuf, in64, s64, hid, act, out64,
+    ss_w, rs_w, ss_s, rs_s, ss_q, rs_q, ss_y, rs_y, ss_z, rs_z, ss_h, rs_h, ss_g, rs_g, lsem,
 ):
     dp, tn = lax.axis_index("dp"), lax.axis_index("tensor")
     x, z, c = dp // 4, (dp // 2) % 2, dp % 2
@@ -174,6 +205,8 @@
         "xm": (at(xm, z, c), tn),
         "z": (at(x, 1 - z, c), tn),
         "sib": (at(x, z, 1 - c), tn),
+        "cross": (at(x, 1 - z, c), (1 - zh) * 4 + y),
+        "peer": (dp, (1 - zh) * 4 + y),
     }
 
     loads = []
@@ -184,36 +217,68 @@
         cp.start()
         return cp
 
-    own = load(w_hbm, w.at[:, pl.ds(0, COLS)])
+    kept = pl.multiple_of((5 + z) * BLOCK, BLOCK)
+    given = pl.multiple_of((6 - z) * BLOCK, BLOCK)
+    plain = (N - 2) * BLOCK
+    own = [
+        load(w_hbm.at[pl.ds(kept, BLOCK)], w.at[pl.ds(0, BLOCK), pl.ds(0, COLS)]),
+        load(w_hbm.at[pl.ds(given, BLOCK)], give_w),
+        load(w_hbm.at[pl.ds(0, plain)], w.at[pl.ds(BLOCK, plain), pl.ds(0, COLS)]),
+    ]
 
     barrier = pltpu.get_barrier_semaphore()
-    for i in range(1, 16):
-        pl.semaphore_signal(barrier, inc=1, device_id=((dp + i) % 16, tn), device_id_type=MESH)
+    for name in ("xp", "xm", "z", "sib", "cross"):
+        pl.semaphore_signal(barrier, inc=1, device_id=dev[name], device_id_type=MESH)
     for i in range(1, 8):
         pl.semaphore_signal(barrier, inc=1, device_id=(dp, (tn + i) % 8), device_id_type=MESH)
 
+    def quarter(i):
+        return pl.ds(i * SLOTS, SLOTS)
+
+    load_give = [load(gate_hbm.at[quarter(i), pl.ds(given, BLOCK)], give_gate.at[quarter(i)]) for i in range(4)]
     load_li = load(li_hbm, li)
     load_sin = load(sin_hbm, sin)
-    load_q = load(q_hbm, qbuf.at[dp])
-    load_small = [load(bi_hbm, bi), load(bo_hbm, bo), load(ev_hbm, ev), load(shid_hbm, shid)]
+    q_me = c * 8 + z * 4 + x
+    load_q = load(q_hbm, qbuf.at[q_me])
+    load_small = [load(bi_hbm, bi), load(bo_hbm, bo), load(ev_hbm, ev)]
+    load_shid = [
+        load(shid_hbm.at[:, pl.ds(kept, BLOCK)], shid.at[:, pl.ds(0, BLOCK)]),
+        load(shid_hbm.at[:, pl.ds(0, plain)], shid.at[:, pl.ds(BLOCK, plain)]),
+    ]
     load_c = []
     for half in range(2):
         cc = c if half == 0 else 1 - c
+        far = (x + 2) % 4
         for slot, (xx, zz) in enumerate(
-            ((x, z), (xm, z), (xp, z), (x, 1 - z), ((x + 2) % 4, z), (xm, 1 - z), (xp, 1 - z), ((x + 2) % 4, 1 - z))
+            ((x, z), (xm, z), (xp, z), (far, z), (x, 1 - z), (xm, 1 - z), (xp, 1 - z), (far, 1 - z))
         ):
             first = pl.multiple_of(at(xx, zz, cc) * COLS, COLS)
-            load_c.append(load(ct_hbm.at[:, pl.ds(first, COLS)], ct.at[:, pl.ds(sibling_column(column(slot)) if half else column(slot), COLS)]))
-    load_gate = load(gate_hbm, gate)
-
-    pl.semaphore_wait(barrier, 22)
+            col = sibling_column(column(slot)) if half else column(slot)
+            load_c.append(load(ct_hbm.at[:, pl.ds(first, COLS)], ct.at[:, pl.ds(col, COLS)]))
+    load_gate = [
+        load(gate_hbm.at[:, pl.ds(kept, BLOCK)], gate.at[:, pl.ds(0, BLOCK)]),
+        load(gate_hbm.at[:, pl.ds(0, plain)], gate.at[:, pl.ds(BLOCK, plain)]),
+    ]
+
+    pl.semaphore_wait(barrier, 12)
 
     def remote(stage, i):
-        src, low, high, to, dst = copies(stage)[i]
-        rows = pl.ds(stage * BLOCK + low, high - low)
-        return pltpu.make_async_remote_copy(
-            src_ref=w.at[rows, pl.ds(column(src), COLS)], dst_ref=w.at[rows, pl.ds(column(dst), COLS)],
-            send_sem=ss_w.at[stage, i], recv_sem=rs_w.at[stage, i],
+        if stage == GATES:
+            rows = quarter(i % 4)
+            to = ("cross", "z")[i // 4]
+            src = (give_gate, relay)[i // 4].at[rows]
+            dst = (relay.at[rows], gate.at[rows, pl.ds(PEER * BLOCK, BLOCK)])[i // 4]
+        else:
+            piece, low, high, to, there = copies(stage)[i]
+            from_rows = pl.ds((0 if stage == PEER else stage * BLOCK) + low, high - low)
+            rows = pl.ds(stage * BLOCK + low, high - low)
+            cols = 3 * COLS if stage == PEER and i >= 2 else COLS
+            src = w.at[from_rows, pl.ds(column(piece), cols)]
+            if stage == 0 and i == 2:
+                src = give_w
+            dst = w.at[rows, pl.ds(column(there), cols)]
+        return pltpu.make_async_remote_copy(
+            src_ref=src, dst_ref=dst, send_sem=ss_w.at[stage, i], recv_sem=rs_w.at[stage, i],
             device_id=dev[to], device_id_type=MESH,
         )
 
@@ -232,7 +297,7 @@
     def sent(stage):
         for i in range(len(copies(stage))):
             remote(stage, i).wait_send()
-        for group in range(3):
+        for group in range(3 if stage < N else 0):
             share_copy(stage, group).wait_send()
 
     row8 = lax.broadcasted_iota(jnp.int32, (8, 128), 0)
@@ -245,11 +310,33 @@
     by_a_t = (row_t % 64 // 8 == col_t).astype(F32)
     dot = functools.partial(jnp.dot, precision=HIGH, preferred_element_type=F32)
 
-    def query_copy(i, owner):
-        return pltpu.make_async_remote_copy(
-            src_ref=q_hbm, dst_ref=qbuf.at[owner], send_sem=ss_q.at[i], recv_sem=rs_q.at[owner],
-            device_id=((dp + i) % 16, tn), device_id_type=MESH,
-        )
+    def query_copy(i, receiving=False):
+        mine = c * 8 + z * 4
+        src, dst, to = (
+            (q_hbm, qbuf.at[mine + (xm if receiving else x)], "xp"),
+            (q_hbm, qbuf.at[mine + (xp if receiving else x)], "xm"),
+            (qbuf.at[mine + xm], qbuf.at[mine + ((x + 2) % 4 if receiving else xm)], "xp"),
+            (qbuf.at[pl.ds(mine, 4)], qbuf.at[pl.ds(c * 8 + (1 - z) * 4 if receiving else mine, 4)], "z"),
+            (qbuf.at[pl.ds(c * 8, 8)], qbuf.at[pl.ds((1 - c) * 8 if receiving else c * 8, 8)], "sib"),
+        )[i]
+        return pltpu.make_async_remote_copy(
+            src_ref=src, dst_ref=dst, send_sem=ss_q.at[i], recv_sem=rs_q.at[i],
+            device_id=dev[to], device_id_type=MESH,
+        )
+
+    def query_far():
+        query_copy(0, True).wait_recv()
+        query_copy(2).start()
+
+    def query_z():
+        query_copy(1, True).wait_recv()
+        query_copy(2, True).wait_recv()
+        load_q.wait()
+        query_copy(3).start()
+
+    def query_sibling():
+        query_copy(3, True).wait_recv()
+        query_copy(4).start()
 
     def y_copy(i, owner):
         return pltpu.make_async_remote_copy(
@@ -263,9 +350,11 @@
             device_id=(dp, (1 - zh) * 4 + y), device_id_type=MESH,
         )
 
-    def send_queries():
-        for i in range(1, 16):
-            query_copy(i, dp).start()
+    def signs_copy():
+        return pltpu.make_async_remote_copy(
+            src_ref=shid_hbm.at[:, pl.ds(given, BLOCK)], dst_ref=shid.at[:, pl.ds(PEER * BLOCK, BLOCK)],
+            send_sem=ss_h, recv_sem=rs_h, device_id=dev["peer"], device_id_type=MESH,
+        )
 
     def input_part():
         load_li.wait()
@@ -293,18 +382,19 @@
             in64[pl.ds(e * SLOTS, SLOTS), :] = dot(part.T, by_a)
 
     def hidden_signs():
-        load_small[3].wait()
+        for cp in load_shid:
+            cp.wait()
+        signs_copy().wait_recv()
         sign = (2 * shid[...] - 1).astype(F32)
         s64[...] = jnp.dot(by_b_t.astype(BF16), sign.astype(BF16), preferred_element_type=F32).astype(BF16)
 
     def query_matrix():
-        for cp in load_small[:3]:
+        for cp in load_small:
             cp.wait()
-        load_q.wait()
-        for i in range(1, 16):
-            query_copy(i, (dp + i) % 16).wait_recv()
+        query_copy(4, True).wait_recv()
         for i in range(16):
-            qfull[pl.ds(4 * i, 4), :] = qbuf[i]
+            owner = i % 4 * 4 + i // 4 % 2 * 2 + i // 8
+            qfull[pl.ds(4 * owner, 4), :] = qbuf[i]
         kron = dot(dot(by_a_t, bi[...]), by_a[:, :64]) * dot(dot(by_b_t, bo[...]), by_b[:, :64])
         values = jnp.sum(dot(ev[...], by_b[:, :64]) * by_a[:, :64], axis=0, keepdims=True)
         both = lax.dot_general(kron / (values + SHIFT), kron[:64], NT, precision=HIGH, preferred_element_type=F32)
@@ -317,38 +407,39 @@
 
     def first_part(j):
         rows = pl.ds(pl.multiple_of(j * BLOCK, BLOCK), BLOCK)
-        hid[j % 4] = lax.dot_general(
+        hid[j] = lax.dot_general(
             ct[:, pl.ds(0, 2560)], w[rows, pl.ds(0, 2560)], NT, preferred_element_type=F32
         )
         g = gate[:, rows].astype(F32)
-        act[j % 4] = g * (0.5 + 0.5 * jnp.tanh(0.5 * g))
+        act[j] = g * (0.5 + 0.5 * jnp.tanh(0.5 * g))
 
     def second_part(j):
         rows = pl.ds(pl.multiple_of(j * BLOCK, BLOCK), BLOCK)
-        product = hid[j % 4] + lax.dot_general(
+        product = hid[j] + lax.dot_general(
             ct[:, pl.ds(2560, 1536)], w[rows, pl.ds(2560, 1536)], NT, preferred_element_type=F32
         )
-        up = (product * act[j % 4]).astype(BF16)
+        up = (product * act[j]).astype(BF16)
         out64[...] += lax.dot_general(up, s64[:, rows], NT, preferred_element_type=F32)
 
     def step_actions(i):
         part, j = SCHEDULE[i][1]
         for arrivals, (what, at, which) in PLAN[i]:
-            for copy in arrivals:
-                remote(at, copy).wait_recv()
+            for stage, copy in arrivals:
+                remote(stage, copy).wait_recv()
             if what == 0:
+                if at == GATES and which < 4:
+                    load_give[which].wait()
                 remote(at, which).start()
             elif what == 1:
                 share_copy(at, which).start()
-            else:
+            elif what == 2:
                 small[at]()
         if i == len(SCHEDULE) - 1:
             for stage in range(5):
                 sent(stage)
-        if part == 0 and j == 0:
-            for cp in load_c:
+        if i == 0:
+            for cp in load_c + load_gate:
                 cp.wait()
-            load_gate.wait()
         for group in ((0,), (1, 2))[part]:
             shared(j, group)
 
@@ -368,12 +459,17 @@
         return 0
 
     def input_start():
-        send_queries()
+        query_copy(0).start()
+        query_copy(1).start()
+        signs_copy().start()
         input_part()
 
-    small = (input_start, hidden_signs, input_sum, input_weigh, query_matrix)
+    small = (
+        input_start, query_far, input_sum, hidden_signs, query_z, input_weigh, query_sibling, query_matrix,
+    )
     out64[...] = jnp.zeros_like(out64)
-    own.wait()
+    for cp in own:
+        cp.wait()
     lax.fori_loop(0, len(SCHEDULE), step, 0)
 
     rows = [
@@ -392,10 +488,11 @@
 
     for i in range(7):
         g_copy(i, tn).start()
-    for stage in range(5, N):
+    for stage in range(5, N + 1):
         sent(stage)
-    for i in range(1, 16):
-        query_copy(i, dp).wait_send()
+    signs_copy().wait_send()
+    for i in range(5):
+        query_copy(i).wait_send()
     for i in range(1, 4):
         y_copy(i, y).wait_send()
     z_copy(zh).wait_send()
@@ -429,6 +526,9 @@
             vmem((HID, D), BF16),
             vmem((TOK, D), BF16),
             vmem((TOK, HID), BF16),
+            vmem((BLOCK, COLS), BF16),
+            vmem((TOK, BLOCK), BF16),
+            vmem((TOK, BLOCK), BF16),
             vmem((TOK, 512), BF16),
             vmem((8, 512), jnp.int32),
             vmem((8, HID), jnp.int32),
@@ -443,11 +543,11 @@
             vmem((8, 8, 128), F32),
             vmem((TOK, 128), F32),
             vmem((128, HID), BF16),
-            vmem((4, TOK, BLOCK), F32),
-            vmem((4, TOK, BLOCK), F32),
+            vmem((N, TOK, BLOCK), F32),
+            vmem((N, TOK, BLOCK), F32),
             vmem((TOK, 128), F32),
-            dma((N, 10)), dma((N, 10)), dma((N, 3)), dma((N, 3)), dma((16,)), dma((16,)),
-            dma((4,)), dma((4,)), dma, dma, dma((8,)), dma((8,)), dma((32,)),
+            dma((N + 1, 10)), dma((N + 1, 10)), dma((N, 3)), dma((N, 3)), dma((5,)), dma((5,)),
+            dma((4,)), dma((4,)), dma, dma, dma, dma, dma((8,)), dma((8,)), dma((40,)),
         ],
         compiler_params=pltpu.CompilerParams(
             collective_id=0, has_side_effects=True, vmem_limit_bytes=56 * 1024 * 1024

time: 70.4 us -> 67.7 us (0.962)
  Pallas kernels: 68.9 us -> 66.3 us
    pallas_call x1, Pallas kernels: 68.9 us -> 66.3 us  [on_device(): pl.pallas_call(kernel, out_shape=jax.ShapeDtypeStruct((4, 512), F32), in_...]
where the time goes in v4:
time: 67.7 us; the launch traced here: 67.6 us
  Pallas kernels  66.3 us (98%)
  local copies, waits for them, and re-layouts  1.3 us (2%)
    pallas_call x1, Pallas kernels, on_device(): pl.pallas_call(kernel, out_shape=jax.ShapeDtypeStruct((4, 512), F32), in_...  66.3 us

profile of v4, /device:TPU:0, one launch (start us, length us, event | category | flops | bytes accessed | tf_op | source)
XLA Modules:
  0.0 67.6 jit_solution(12988954265210292053)
XLA Ops:
  0.0 66.3 %scores.1 = f32[4,512]{1,0:T(4,128)} custom-call(bf16[1024,512]{1,0:T(8,128)(2,1)} %bitcast.8, bf16[1024,4096]{1,0:T(8,128)(2,1)} %bitcast.6, bf16[1024,1792]{1,0:T(8,128)(2,1)} %bitcast.7, bf16[1792,256]{1,0:T(8,128)(2,1)} %w_hbm.1, s32[4]{0:T(128)} %len_ref.1, s32[8,512]{1,0:T(8,128)} %bitcast.10, s32[8,1792]{1,0:T(8,128)} %bitcast.9, f32[8,8]{1,0:T(8,128)} %bi_hbm.1, ...), custom_call_target="tpu_custom_call" | custom-call | flops 15032385536 | bytes 30000000 | tf_op jit(solution)/shard_map/scores/pallas_call | solution.py:520
  66.3 1.3 %copy.13 = f32[4,512]{1,0:T(4,128)} copy(f32[4,512]{1,0:T(4,128)} %scores.1) | data formatting | bytes 16384

commit v5 on v4

--- a/solution.py
+++ b/solution.py
@@ -18,88 +18,83 @@
 
 N = HID // BLOCK
 PEER, GATES = N - 1, N
-ALONG_X = (16, 16, 16, 16, 16)
+ALONG_X = (15, 15, 16, 16, 16)
 SCHEDULE = (
     (
         (
-            (0, 0, 0), (0, 0, 1), (0, 0, 2), (0, 6, 0), (0, 1, 0), (0, 1, 1), (0, 1, 2), (2, 0, 0),
-            (0, 2, 0), (0, 2, 1), (0, 2, 2), (0, 7, 0), (0, 6, 1), (2, 3, 0), (0, 0, 5), (0, 0, 6),
-            (0, 3, 2), (2, 1, 0), (2, 2, 0), (0, 7, 1), (0, 0, 3), (0, 0, 4), (0, 7, 4), (0, 7, 2),
-            (0, 1, 3), (0, 1, 4), (2, 4, 0), (2, 5, 0), (0, 2, 3), (0, 2, 4), (0, 4, 2), (0, 7, 3),
-            (0, 3, 0), (0, 3, 1), (1, 0, 1), (0, 7, 5), (1, 0, 0), (2, 6, 0), (0, 6, 2), (0, 4, 0),
-            (0, 4, 1), (1, 1, 0),
+            (0, 0, 0), (0, 1, 0), (0, 0, 1), (0, 1, 1), (0, 0, 2), (0, 1, 2), (0, 6, 0), (2, 0, 0),
+            (0, 2, 0), (0, 2, 1), (0, 2, 2), (0, 7, 0), (0, 7, 1), (2, 2, 0), (0, 0, 3), (0, 0, 4),
+            (0, 3, 2), (0, 6, 1), (0, 0, 5), (0, 0, 6), (2, 1, 0), (2, 3, 0), (0, 7, 4), (0, 7, 2),
+            (0, 1, 4), (0, 1, 3), (0, 2, 4), (0, 2, 3), (2, 5, 0), (0, 7, 5), (0, 6, 2), (1, 0, 0),
+            (0, 3, 1), (0, 3, 0), (0, 4, 2), (1, 0, 1), (2, 4, 0),
         ),
         (0, 0),
     ),
     (
         (
-            (0, 0, 7), (0, 0, 8), (0, 7, 6), (1, 2, 0),
+            (0, 0, 7), (0, 0, 8), (0, 4, 1), (1, 1, 0), (0, 4, 0), (1, 2, 0), (0, 7, 6),
         ),
         (0, 1),
     ),
     (
         (
-            (0, 3, 3), (0, 3, 4), (0, 7, 7), (2, 7, 0), (0, 5, 0), (0, 5, 1), (0, 5, 2),
+            (0, 3, 3), (0, 5, 0), (0, 3, 4), (0, 5, 1), (0, 1, 7), (0, 7, 3),
         ),
         (0, 2),
     ),
     (
         (
-            (0, 4, 3), (0, 4, 4), (0, 6, 3), (1, 0, 2), (0, 1, 5), (0, 1, 6), (0, 1, 7), (1, 3, 0),
+            (0, 6, 3), (1, 0, 2), (0, 5, 2), (2, 6, 0), (0, 1, 6), (0, 1, 5),
         ),
         (1, 0),
     ),
     (
         (
+            (0, 1, 8), (0, 1, 9), (1, 3, 0), (1, 6, 1), (1, 6, 2), (0, 4, 3), (0, 4, 4), (0, 2, 7),
+            (2, 7, 0), (0, 5, 3), (0, 5, 4), (1, 1, 2),
         ),
         (0, 3),
     ),
     (
         (
-            (0, 5, 3), (0, 2, 5), (0, 5, 4), (0, 2, 6), (0, 2, 7), (1, 4, 0), (1, 6, 1), (1, 6, 2),
-            (0, 3, 7), (0, 3, 5), (0, 3, 6), (1, 1, 1), (1, 1, 2),
+            (0, 2, 5), (0, 2, 6), (0, 7, 7), (1, 1, 1), (0, 3, 6), (0, 3, 5), (0, 2, 8), (0, 2, 9),
+            (0, 3, 7), (1, 4, 0),
+        ),
+        (1, 1),
+    ),
+    (
+        (
+            (1, 2, 2), (1, 5, 0), (0, 4, 6), (0, 4, 5),
         ),
         (0, 4),
     ),
     (
         (
-            (0, 4, 7), (1, 5, 0),
-        ),
-        (1, 1),
-    ),
-    (
-        (
-            (0, 4, 5), (0, 4, 6), (1, 2, 2), (1, 6, 0), (1, 2, 1), (0, 5, 7),
+            (0, 4, 7), (1, 6, 0),
         ),
         (0, 5),
     ),
     (
         (
-            (0, 5, 5), (0, 5, 6), (1, 3, 2),
-        ),
-        (0, 6),
-    ),
-    (
-        (
-            (1, 3, 1),
-        ),
-        (1, 6),
-    ),
-    (
-        (
-            (1, 4, 2), (1, 4, 1),
+            (0, 5, 5), (0, 5, 6), (0, 5, 7), (1, 2, 1),
+        ),
+        (2, 6),
+    ),
+    (
+        (
+            (1, 3, 1), (1, 3, 2), (1, 4, 1),
         ),
         (1, 2),
     ),
     (
         (
-            (1, 5, 2),
+            (1, 4, 2),
         ),
         (1, 3),
     ),
     (
         (
-            (1, 5, 1),
+            (1, 5, 1), (1, 5, 2),
         ),
         (1, 4),
     ),
@@ -170,7 +165,7 @@
                 needed = after(at, which)
             elif what == 1:
                 needed = brought(at, which)
-            elif what == 3 and part == 0 and block == PEER:
+            elif what == 3 and part != 1 and block == PEER:
                 needed = [(GATES, i) for i in range(4, 8)]
             new = [x for x in needed if x not in arrived]
             arrived.update(new)
@@ -179,6 +174,7 @@
 
 
 PLAN = plan()
+EARLY = [what == 0 and at == 0 and not new for new, (what, at, _) in PLAN[0]].index(False)
 
 
 def column(slot):
@@ -209,58 +205,65 @@
         "peer": (dp, (1 - zh) * 4 + y),
     }
 
-    loads = []
-
-    def load(src, dst):
-        cp = pltpu.make_async_copy(src, dst, lsem.at[len(loads)])
-        loads.append(cp)
-        cp.start()
-        return cp
-
     kept = pl.multiple_of((5 + z) * BLOCK, BLOCK)
     given = pl.multiple_of((6 - z) * BLOCK, BLOCK)
     plain = (N - 2) * BLOCK
-    own = [
-        load(w_hbm.at[pl.ds(kept, BLOCK)], w.at[pl.ds(0, BLOCK), pl.ds(0, COLS)]),
-        load(w_hbm.at[pl.ds(given, BLOCK)], give_w),
-        load(w_hbm.at[pl.ds(0, plain)], w.at[pl.ds(BLOCK, plain), pl.ds(0, COLS)]),
-    ]
-
+    q_me = c * 8 + z * 4 + x
+
+    def quarter(i):
+        return pl.ds(i * SLOTS, SLOTS)
+
+    def loads():
+        found, count = {}, 0
+
+        def load(name, src, dst):
+            nonlocal count
+            found.setdefault(name, []).append(functools.partial(pltpu.make_async_copy, src, dst, lsem.at[count]))
+            count += 1
+
+        load("own", w_hbm.at[pl.ds(kept, BLOCK)], w.at[pl.ds(0, BLOCK), pl.ds(0, COLS)])
+        load("own", w_hbm.at[pl.ds(given, BLOCK)], give_w)
+        load("plain", w_hbm.at[pl.ds(0, plain)], w.at[pl.ds(BLOCK, plain), pl.ds(0, COLS)])
+        for i in range(4):
+            load("give", gate_hbm.at[quarter(i), pl.ds(given, BLOCK)], give_gate.at[quarter(i)])
+        load("input", li_hbm, li)
+        load("input", sin_hbm, sin)
+        load("query", q_hbm, qbuf.at[q_me])
+        load("signs", shid_hbm.at[:, pl.ds(kept, BLOCK)], shid.at[:, pl.ds(0, BLOCK)])
+        load("signs", shid_hbm.at[:, pl.ds(0, plain)], shid.at[:, pl.ds(BLOCK, plain)])
+        for half in range(2):
+            cc = c if half == 0 else 1 - c
+            far = (x + 2) % 4
+            for slot, (xx, zz) in enumerate(
+                ((x, z), (xm, z), (xp, z), (far, z), (x, 1 - z), (xm, 1 - z), (xp, 1 - z), (far, 1 - z))
+            ):
+                first = pl.multiple_of(at(xx, zz, cc) * COLS, COLS)
+                col = sibling_column(column(slot)) if half else column(slot)
+                load("c", ct_hbm.at[:, pl.ds(first, COLS)], ct.at[:, pl.ds(col, COLS)])
+        load("gate", gate_hbm.at[:, pl.ds(kept, BLOCK)], gate.at[:, pl.ds(0, BLOCK)])
+        load("gate", gate_hbm.at[:, pl.ds(0, plain)], gate.at[:, pl.ds(BLOCK, plain)])
+        for src, dst in ((bi_hbm, bi), (bo_hbm, bo), (ev_hbm, ev)):
+            load("small", src, dst)
+        return found
+
+    def start(*names):
+        for name in names:
+            for make in loads()[name]:
+                make().start()
+
+    def loaded(*names):
+        for name in names:
+            for make in loads()[name]:
+                make().wait()
+
+    start("own", "plain")
     barrier = pltpu.get_barrier_semaphore()
     for name in ("xp", "xm", "z", "sib", "cross"):
         pl.semaphore_signal(barrier, inc=1, device_id=dev[name], device_id_type=MESH)
     for i in range(1, 8):
         pl.semaphore_signal(barrier, inc=1, device_id=(dp, (tn + i) % 8), device_id_type=MESH)
-
-    def quarter(i):
-        return pl.ds(i * SLOTS, SLOTS)
-
-    load_give = [load(gate_hbm.at[quarter(i), pl.ds(given, BLOCK)], give_gate.at[quarter(i)]) for i in range(4)]
-    load_li = load(li_hbm, li)
-    load_sin = load(sin_hbm, sin)
-    q_me = c * 8 + z * 4 + x
-    load_q = load(q_hbm, qbuf.at[q_me])
-    load_small = [load(bi_hbm, bi), load(bo_hbm, bo), load(ev_hbm, ev)]
-    load_shid = [
-        load(shid_hbm.at[:, pl.ds(kept, BLOCK)], shid.at[:, pl.ds(0, BLOCK)]),
-        load(shid_hbm.at[:, pl.ds(0, plain)], shid.at[:, pl.ds(BLOCK, plain)]),
-    ]
-    load_c = []
-    for half in range(2):
-        cc = c if half == 0 else 1 - c
-        far = (x + 2) % 4
-        for slot, (xx, zz) in enumerate(
-            ((x, z), (xm, z), (xp, z), (far, z), (x, 1 - z), (xm, 1 - z), (xp, 1 - z), (far, 1 - z))
-        ):
-            first = pl.multiple_of(at(xx, zz, cc) * COLS, COLS)
-            col = sibling_column(column(slot)) if half else column(slot)
-            load_c.append(load(ct_hbm.at[:, pl.ds(first, COLS)], ct.at[:, pl.ds(col, COLS)]))
-    load_gate = [
-        load(gate_hbm.at[:, pl.ds(kept, BLOCK)], gate.at[:, pl.ds(0, BLOCK)]),
-        load(gate_hbm.at[:, pl.ds(0, plain)], gate.at[:, pl.ds(BLOCK, plain)]),
-    ]
-
     pl.semaphore_wait(barrier, 12)
+    loaded("own")
 
     def remote(stage, i):
         if stage == GATES:
@@ -331,7 +334,7 @@
     def query_z():
         query_copy(1, True).wait_recv()
         query_copy(2, True).wait_recv()
-        load_q.wait()
+        loaded("query")
         query_copy(3).start()
 
     def query_sibling():
@@ -357,8 +360,7 @@
         )
 
     def input_part():
-        load_li.wait()
-        load_sin.wait()
+        loaded("input")
         sign = (2 * sin[...] - 1).astype(F32).astype(BF16)
         ybuf[y] = lax.dot_general(sign, li[...], NT, preferred_element_type=F32) * D ** (-0.5)
         for i in range(1, 4):
@@ -382,15 +384,13 @@
             in64[pl.ds(e * SLOTS, SLOTS), :] = dot(part.T, by_a)
 
     def hidden_signs():
-        for cp in load_shid:
-            cp.wait()
+        loaded("signs")
         signs_copy().wait_recv()
         sign = (2 * shid[...] - 1).astype(F32)
         s64[...] = jnp.dot(by_b_t.astype(BF16), sign.astype(BF16), preferred_element_type=F32).astype(BF16)
 
     def query_matrix():
-        for cp in load_small:
-            cp.wait()
+        loaded("small")
         query_copy(4, True).wait_recv()
         for i in range(16):
             owner = i % 4 * 4 + i // 4 % 2 * 2 + i // 8
@@ -405,30 +405,44 @@
         mat[pl.ds(0, 128), :] = both_parts
         mat[pl.ds(128, 128), :] = both_parts
 
+    def activation(rows):
+        g = gate[:, rows].astype(F32)
+        return g * (0.5 + 0.5 * jnp.tanh(0.5 * g))
+
+    def project(rows, product, factor):
+        up = (product * factor).astype(BF16)
+        out64[...] += lax.dot_general(up, s64[:, rows], NT, preferred_element_type=F32)
+
     def first_part(j):
         rows = pl.ds(pl.multiple_of(j * BLOCK, BLOCK), BLOCK)
         hid[j] = lax.dot_general(
             ct[:, pl.ds(0, 2560)], w[rows, pl.ds(0, 2560)], NT, preferred_element_type=F32
         )
-        g = gate[:, rows].astype(F32)
-        act[j] = g * (0.5 + 0.5 * jnp.tanh(0.5 * g))
+        act[j] = activation(rows)
 
     def second_part(j):
         rows = pl.ds(pl.multiple_of(j * BLOCK, BLOCK), BLOCK)
         product = hid[j] + lax.dot_general(
             ct[:, pl.ds(2560, 1536)], w[rows, pl.ds(2560, 1536)], NT, preferred_element_type=F32
         )
-        up = (product * act[j]).astype(BF16)
-        out64[...] += lax.dot_general(up, s64[:, rows], NT, preferred_element_type=F32)
+        project(rows, product, act[j])
+
+    def whole(j):
+        rows = pl.ds(pl.multiple_of(j * BLOCK, BLOCK), BLOCK)
+        product = lax.dot_general(ct[...], w[rows, :], NT, preferred_element_type=F32)
+        project(rows, product, activation(rows))
 
     def step_actions(i):
         part, j = SCHEDULE[i][1]
-        for arrivals, (what, at, which) in PLAN[i]:
+        for n, (arrivals, (what, at, which)) in enumerate(PLAN[i]):
+            if i == 0 and n == EARLY:
+                start("give", "input", "query", "signs", "c", "gate", "small")
+                loaded("plain")
             for stage, copy in arrivals:
                 remote(stage, copy).wait_recv()
             if what == 0:
                 if at == GATES and which < 4:
-                    load_give[which].wait()
+                    loads()["give"][which]().wait()
                 remote(at, which).start()
             elif what == 1:
                 share_copy(at, which).start()
@@ -438,9 +452,8 @@
             for stage in range(5):
                 sent(stage)
         if i == 0:
-            for cp in load_c + load_gate:
-                cp.wait()
-        for group in ((0,), (1, 2))[part]:
+            loaded("c", "gate")
+        for group in ((0,), (1, 2), (0, 1, 2))[part]:
             shared(j, group)
 
     def block_of(step, part):
@@ -453,9 +466,9 @@
     def step(k, _):
         for i in range(len(SCHEDULE)):
             pl.when(k == i)(functools.partial(step_actions, i))
-        first, second = block_of(k, 0), block_of(k, 1)
-        pl.when(first >= 0)(lambda: first_part(first))
-        pl.when(second >= 0)(lambda: second_part(second))
+        for part, compute in enumerate((first_part, second_part, whole)):
+            j = block_of(k, part)
+            pl.when(j >= 0)(functools.partial(compute, j))
         return 0
 
     def input_start():
@@ -468,8 +481,6 @@
         input_start, query_far, input_sum, hidden_signs, query_z, input_weigh, query_sibling, query_matrix,
     )
     out64[...] = jnp.zeros_like(out64)
-    for cp in own:
-        cp.wait()
     lax.fori_loop(0, len(SCHEDULE), step, 0)
 
     rows = [
@@ -519,7 +530,7 @@
     specs[4] = pl.BlockSpec(memory_space=pltpu.SMEM)
     return pl.pallas_call(
         kernel,
-        out_shape=jax.ShapeDtypeStruct((4, 512), F32),
+        out_shape=pltpu.VMEM((4, 512), F32),
         in_specs=specs,
         out_specs=pl.BlockSpec(memory_space=pltpu.VMEM),
         scratch_shapes=[

time: 67.7 us -> 65.9 us (0.973)
  Pallas kernels: 66.3 us -> 64.6 us
  local copies, waits for them, and re-layouts: 1.3 us -> 0.6 us
    pallas_call x1, Pallas kernels: 66.3 us -> 64.6 us  [on_device(): pl.pallas_call(kernel, out_shape=pltpu.VMEM((4, 512), F32), in_specs=spec...]
    unnamed x1, local copies, waits for them, and re-layouts: 1.3 us -> 0.6 us
where the time goes in v5:
time: 65.9 us; the launch traced here: 65.2 us
  Pallas kernels  64.6 us (98%)
    pallas_call x1, Pallas kernels, on_device(): pl.pallas_call(kernel, out_shape=pltpu.VMEM((4, 512), F32), in_specs=spec...  64.6 us

profile of v5, /device:TPU:0, one launch (start us, length us, event | category | flops | bytes accessed | tf_op | source)
XLA Modules:
  0.0 65.2 jit_solution(13753189428183759181)
XLA Ops:
  0.0 64.6 %scores.1 = f32[4,512]{1,0:T(4,128)S(1)} custom-call(bf16[1024,512]{1,0:T(8,128)(2,1)} %bitcast.8, bf16[1024,4096]{1,0:T(8,128)(2,1)} %bitcast.6, bf16[1024,1792]{1,0:T(8,128)(2,1)} %bitcast.7, bf16[1792,256]{1,0:T(8,128)(2,1)} %w_hbm.1, s32[4]{0:T(128)} %len_ref.1, s32[8,512]{1,0:T(8,128)} %bitcast.10, s32[8,1792]{1,0:T(8,128)} %bitcast.9, f32[8,8]{1,0:T(8,128)} %bi_hbm.1, ...), custom_call_target="tpu_custom_call" | custom-call | flops 15032385536 | bytes 30000000 | tf_op jit(solution)/shard_map/scores/pallas_call | solution.py:531
  64.6 0.6 copy.13

commit v6 on v5

--- a/solution.py
+++ b/solution.py
@@ -155,6 +155,23 @@
     return [(stage, i) for i in which if i < len(copies(stage))]
 
 
+def bundle(stage, i):
+    if stage == PEER:
+        return (0, 0, 1, 0)[i]
+    if stage == GATES:
+        return min(i, 4)
+    if stage == 0:
+        return (0, 1, 2, 3, 3, 4, 4, 5, 5)[i]
+    return (0, 1, 2, 3, 3, 4, 4, 5, 4, 4)[i]
+
+
+def receive_sem(stage, which):
+    return stage * 6 + which if stage <= PEER else PEER * 6 + 2 + which
+
+
+RECEIVE_SEMS = PEER * 6 + 2 + 5
+
+
 def plan():
     arrived, steps = set(), []
     for actions, (part, block) in SCHEDULE:
@@ -167,13 +184,16 @@
                 needed = brought(at, which)
             elif what == 3 and part != 1 and block == PEER:
                 needed = [(GATES, i) for i in range(4, 8)]
-            new = [x for x in needed if x not in arrived]
+            new = sorted({(at, bundle(at, i)) for at, i in needed} - arrived)
             arrived.update(new)
             steps[-1].append((new, (what, at, which)))
     return steps
 
 
 PLAN = plan()
+GIVE_FIRST = min(
+    (i, n) for i, step in enumerate(PLAN) for n, (_, (what, at, which)) in enumerate(step) if (what, at) == (0, GATES) and which < 4
+)
 EARLY = [what == 0 and at == 0 and not new for new, (what, at, _) in PLAN[0]].index(False)
 
 
@@ -189,7 +209,7 @@
     li_hbm, ct_hbm, gate_hbm, w_hbm, len_ref, sin_hbm, shid_hbm, bi_hbm, bo_hbm, ev_hbm, q_hbm,
     o_ref,
     w, ct, gate, give_w, give_gate, relay, li, sin, shid, bi, bo, ev, qbuf, qfull, mat, ybuf, zbuf, gbuf, in64, s64, hid, act, out64,
-    ss_w, rs_w, ss_s, rs_s, ss_q, rs_q, ss_y, rs_y, ss_z, rs_z, ss_h, rs_h, ss_g, rs_g, lsem,
+    ss_w, rs_w, ss_s, rs_s, ss_q, rs_q, ss_y, rs_y, rs_z, ss_h, rs_h, ss_g, rs_g, lsem,
 ):
     dp, tn = lax.axis_index("dp"), lax.axis_index("tensor")
     x, z, c = dp // 4, (dp // 2) % 2, dp % 2
@@ -213,48 +233,63 @@
     def quarter(i):
         return pl.ds(i * SLOTS, SLOTS)
 
-    def loads():
-        found, count = {}, 0
-
-        def load(name, src, dst):
-            nonlocal count
-            found.setdefault(name, []).append(functools.partial(pltpu.make_async_copy, src, dst, lsem.at[count]))
-            count += 1
-
-        load("own", w_hbm.at[pl.ds(kept, BLOCK)], w.at[pl.ds(0, BLOCK), pl.ds(0, COLS)])
-        load("own", w_hbm.at[pl.ds(given, BLOCK)], give_w)
-        load("plain", w_hbm.at[pl.ds(0, plain)], w.at[pl.ds(BLOCK, plain), pl.ds(0, COLS)])
-        for i in range(4):
-            load("give", gate_hbm.at[quarter(i), pl.ds(given, BLOCK)], give_gate.at[quarter(i)])
-        load("input", li_hbm, li)
-        load("input", sin_hbm, sin)
-        load("query", q_hbm, qbuf.at[q_me])
-        load("signs", shid_hbm.at[:, pl.ds(kept, BLOCK)], shid.at[:, pl.ds(0, BLOCK)])
-        load("signs", shid_hbm.at[:, pl.ds(0, plain)], shid.at[:, pl.ds(BLOCK, plain)])
+    def done(ref, sem):
+        pltpu.make_async_copy(ref, ref, sem).wait()
+
+    NAMES = ("own", "plain", "give", "input", "insigns", "query", "signs", "c", "gate", "bi", "bo", "ev")
+
+    def start(*names):
+        for name in names:
+            for src, dst in copies_in[name]():
+                pltpu.make_async_copy(src, dst, lsem.at[NAMES.index(name)]).start()
+
+    def loaded(*names):
+        whole_of = {
+            "own": w.at[pl.ds(0, 2 * BLOCK), pl.ds(0, COLS)],
+            "plain": w.at[pl.ds(BLOCK, plain), pl.ds(0, COLS)],
+            "give": give_gate, "input": li, "insigns": sin, "query": qbuf.at[q_me],
+            "signs": shid.at[:, pl.ds(0, plain + BLOCK)], "c": ct, "gate": gate.at[:, pl.ds(0, plain + BLOCK)],
+            "bi": bi, "bo": bo, "ev": ev,
+        }
+        for name in names:
+            done(whole_of[name], lsem.at[NAMES.index(name)])
+
+    def load_c():
+        found = []
+        far = (x + 2) % 4
         for half in range(2):
             cc = c if half == 0 else 1 - c
-            far = (x + 2) % 4
             for slot, (xx, zz) in enumerate(
                 ((x, z), (xm, z), (xp, z), (far, z), (x, 1 - z), (xm, 1 - z), (xp, 1 - z), (far, 1 - z))
             ):
                 first = pl.multiple_of(at(xx, zz, cc) * COLS, COLS)
                 col = sibling_column(column(slot)) if half else column(slot)
-                load("c", ct_hbm.at[:, pl.ds(first, COLS)], ct.at[:, pl.ds(col, COLS)])
-        load("gate", gate_hbm.at[:, pl.ds(kept, BLOCK)], gate.at[:, pl.ds(0, BLOCK)])
-        load("gate", gate_hbm.at[:, pl.ds(0, plain)], gate.at[:, pl.ds(BLOCK, plain)])
-        for src, dst in ((bi_hbm, bi), (bo_hbm, bo), (ev_hbm, ev)):
-            load("small", src, dst)
+                found.append((ct_hbm.at[:, pl.ds(first, COLS)], ct.at[:, pl.ds(col, COLS)]))
         return found
 
-    def start(*names):
-        for name in names:
-            for make in loads()[name]:
-                make().start()
-
-    def loaded(*names):
-        for name in names:
-            for make in loads()[name]:
-                make().wait()
+    def by_place(src, dst):
+        return [
+            (src.at[:, pl.ds(kept, BLOCK)], dst.at[:, pl.ds(0, BLOCK)]),
+            (src.at[:, pl.ds(0, plain)], dst.at[:, pl.ds(BLOCK, plain)]),
+        ]
+
+    copies_in = {
+        "own": lambda: [
+            (w_hbm.at[pl.ds(kept, BLOCK)], w.at[pl.ds(0, BLOCK), pl.ds(0, COLS)]),
+            (w_hbm.at[pl.ds(given, BLOCK)], give_w),
+        ],
+        "plain": lambda: [(w_hbm.at[pl.ds(0, plain)], w.at[pl.ds(BLOCK, plain), pl.ds(0, COLS)])],
+        "give": lambda: [(gate_hbm.at[:, pl.ds(given, BLOCK)], give_gate)],
+        "input": lambda: [(li_hbm, li)],
+        "insigns": lambda: [(sin_hbm, sin)],
+        "query": lambda: [(q_hbm, qbuf.at[q_me])],
+        "signs": lambda: by_place(shid_hbm, shid),
+        "c": load_c,
+        "gate": lambda: by_place(gate_hbm, gate),
+        "bi": lambda: [(bi_hbm, bi)],
+        "bo": lambda: [(bo_hbm, bo)],
+        "ev": lambda: [(ev_hbm, ev)],
+    }
 
     start("own", "plain")
     barrier = pltpu.get_barrier_semaphore()
@@ -281,27 +316,33 @@
                 src = give_w
             dst = w.at[rows, pl.ds(column(there), cols)]
         return pltpu.make_async_remote_copy(
-            src_ref=src, dst_ref=dst, send_sem=ss_w.at[stage, i], recv_sem=rs_w.at[stage, i],
+            src_ref=src, dst_ref=dst, send_sem=ss_w, recv_sem=rs_w.at[receive_sem(stage, bundle(stage, i))],
             device_id=dev[to], device_id_type=MESH,
         )
+
+    def arrive(stage, which):
+        if stage == GATES:
+            ref = relay.at[quarter(which)] if which < 4 else gate.at[:, pl.ds(PEER * BLOCK, BLOCK)]
+        else:
+            if stage == PEER:
+                col, cols = ((0, 5 * COLS), (column(ZL), 3 * COLS))[which]
+            else:
+                col, cols = (column((L, R, Z, FAR, ZL, ZF)[which]), 2 * COLS if which == 4 else COLS)
+            ref = w.at[pl.ds(stage * BLOCK, BLOCK), pl.ds(col, cols)]
+        done(ref, rs_w.at[receive_sem(stage, which)])
 
     def share_copy(stage, group):
         rows = pl.ds(stage * BLOCK, BLOCK)
         col, cols = GROUPS[group]
         return pltpu.make_async_remote_copy(
             src_ref=w.at[rows, pl.ds(col, cols)], dst_ref=w.at[rows, pl.ds(sibling_column(col), cols)],
-            send_sem=ss_s.at[stage, group], recv_sem=rs_s.at[stage, group],
+            send_sem=ss_s, recv_sem=rs_s.at[stage, min(group, 1)],
             device_id=dev["sib"], device_id_type=MESH,
         )
 
-    def shared(stage, group):
-        share_copy(stage, group).wait_recv()
-
-    def sent(stage):
-        for i in range(len(copies(stage))):
-            remote(stage, i).wait_send()
-        for group in range(3 if stage < N else 0):
-            share_copy(stage, group).wait_send()
+    def shared(stage, part):
+        col, cols = ((0, 1280), (2560, 768))[part]
+        done(w.at[pl.ds(stage * BLOCK, BLOCK), pl.ds(sibling_column(col), cols)], rs_s.at[stage, part])
 
     row8 = lax.broadcasted_iota(jnp.int32, (8, 128), 0)
     col8 = lax.broadcasted_iota(jnp.int32, (8, 128), 1)
@@ -323,7 +364,7 @@
             (qbuf.at[pl.ds(c * 8, 8)], qbuf.at[pl.ds((1 - c) * 8 if receiving else c * 8, 8)], "sib"),
         )[i]
         return pltpu.make_async_remote_copy(
-            src_ref=src, dst_ref=dst, send_sem=ss_q.at[i], recv_sem=rs_q.at[i],
+            src_ref=src, dst_ref=dst, send_sem=ss_q, recv_sem=rs_q.at[(0, 1, 1, 2, 3)[i]],
             device_id=dev[to], device_id_type=MESH,
         )
 
@@ -332,8 +373,7 @@
         query_copy(2).start()
 
     def query_z():
-        query_copy(1, True).wait_recv()
-        query_copy(2, True).wait_recv()
+        done(qbuf.at[pl.ds(c * 8 + z * 4, 2)], rs_q.at[1])
         loaded("query")
         query_copy(3).start()
 
@@ -343,13 +383,13 @@
 
     def y_copy(i, owner):
         return pltpu.make_async_remote_copy(
-            src_ref=ybuf.at[owner], dst_ref=ybuf.at[owner], send_sem=ss_y.at[i], recv_sem=rs_y.at[owner],
+            src_ref=ybuf.at[owner], dst_ref=ybuf.at[owner], send_sem=ss_y, recv_sem=rs_y,
             device_id=(dp, zh * 4 + (y + i) % 4), device_id_type=MESH,
         )
 
     def z_copy(owner):
         return pltpu.make_async_remote_copy(
-            src_ref=zbuf.at[owner], dst_ref=zbuf.at[owner], send_sem=ss_z, recv_sem=rs_z,
+            src_ref=zbuf.at[owner], dst_ref=zbuf.at[owner], send_sem=ss_y, recv_sem=rs_z,
             device_id=(dp, (1 - zh) * 4 + y), device_id_type=MESH,
         )
 
@@ -360,15 +400,14 @@
         )
 
     def input_part():
-        loaded("input")
+        loaded("input", "insigns")
         sign = (2 * sin[...] - 1).astype(F32).astype(BF16)
         ybuf[y] = lax.dot_general(sign, li[...], NT, preferred_element_type=F32) * D ** (-0.5)
         for i in range(1, 4):
             y_copy(i, y).start()
 
     def input_sum():
-        for i in range(1, 4):
-            y_copy(i, (y + i) % 4).wait_recv()
+        done(ybuf.at[pl.ds(0, 3)], rs_y)
         zbuf[zh] = ybuf[0] + ybuf[1] + ybuf[2] + ybuf[3]
         z_copy(zh).start()
 
@@ -390,7 +429,7 @@
         s64[...] = jnp.dot(by_b_t.astype(BF16), sign.astype(BF16), preferred_element_type=F32).astype(BF16)
 
     def query_matrix():
-        loaded("small")
+        loaded("bi", "bo", "ev")
         query_copy(4, True).wait_recv()
         for i in range(16):
             owner = i % 4 * 4 + i // 4 % 2 * 2 + i // 8
@@ -436,25 +475,22 @@
         part, j = SCHEDULE[i][1]
         for n, (arrivals, (what, at, which)) in enumerate(PLAN[i]):
             if i == 0 and n == EARLY:
-                start("give", "input", "query", "signs", "c", "gate", "small")
+                start("give", "input", "insigns", "query", "signs", "c", "gate", "bi", "bo", "ev")
                 loaded("plain")
             for stage, copy in arrivals:
-                remote(stage, copy).wait_recv()
+                arrive(stage, copy)
             if what == 0:
-                if at == GATES and which < 4:
-                    loads()["give"][which]().wait()
+                if (i, n) == GIVE_FIRST:
+                    loaded("give")
                 remote(at, which).start()
             elif what == 1:
                 share_copy(at, which).start()
             elif what == 2:
                 small[at]()
-        if i == len(SCHEDULE) - 1:
-            for stage in range(5):
-                sent(stage)
         if i == 0:
             loaded("c", "gate")
-        for group in ((0,), (1, 2), (0, 1, 2))[part]:
-            shared(j, group)
+        for half in ((0,), (1,), (0, 1))[part]:
+            shared(j, half)
 
     def block_of(step, part):
         j = jnp.int32(-1)
@@ -493,22 +529,18 @@
 
     def g_copy(i, owner):
         return pltpu.make_async_remote_copy(
-            src_ref=gbuf.at[owner], dst_ref=gbuf.at[owner], send_sem=ss_g.at[i], recv_sem=rs_g.at[owner],
+            src_ref=gbuf.at[owner], dst_ref=gbuf.at[owner], send_sem=ss_g, recv_sem=rs_g,
             device_id=(dp, (zh + 1 - i // 4) % 2 * 4 + (y + FAR_FIRST[i % 4]) % 4), device_id_type=MESH,
         )
 
     for i in range(7):
         g_copy(i, tn).start()
-    for stage in range(5, N + 1):
-        sent(stage)
+    done(w.at[pl.ds(0, 928)], ss_w)
+    done(w.at[:, pl.ds(0, 2048)], ss_s)
+    done(qbuf.at[pl.ds(0, 15)], ss_q)
+    done(ybuf, ss_y)
     signs_copy().wait_send()
-    for i in range(5):
-        query_copy(i).wait_send()
-    for i in range(1, 4):
-        y_copy(i, y).wait_send()
-    z_copy(zh).wait_send()
-    for i in range(1, 8):
-        g_copy(0, (tn + i) % 8).wait_recv()
+    done(gbuf.at[pl.ds(0, 7)], rs_g)
     total = gbuf[0]
     for i in range(1, 8):
         total = total + gbuf[i]
@@ -516,8 +548,7 @@
     rest = (total - top.astype(F32)).astype(BF16)
     both = jnp.concatenate([top, rest], axis=1)
     o_ref[...] = jnp.dot(both, mat[...], preferred_element_type=F32)[:4, :]
-    for i in range(7):
-        g_copy(i, tn).wait_send()
+    done(gbuf.at[pl.ds(0, 7)], ss_g)
 
 
 def on_device(
@@ -557,8 +588,7 @@
             vmem((N, TOK, BLOCK), F32),
             vmem((N, TOK, BLOCK), F32),
             vmem((TOK, 128), F32),
-            dma((N + 1, 10)), dma((N + 1, 10)), dma((N, 3)), dma((N, 3)), dma((5,)), dma((5,)),
-            dma((4,)), dma((4,)), dma, dma, dma, dma, dma((8,)), dma((8,)), dma((40,)),
+            dma, dma((RECEIVE_SEMS,)), dma, dma((N, 2)), dma, dma((4,)), dma, dma, dma, dma, dma, dma, dma, dma((12,)),
         ],
         compiler_params=pltpu.CompilerParams(
             collective_id=0, has_side_effects=True, vmem_limit_bytes=56 * 1024 * 1024

time: 65.9 us -> 63.4 us (0.962)
  Pallas kernels: 64.6 us -> 62.2 us
    pallas_call x1, Pallas kernels: 64.6 us -> 62.2 us  [on_device(): pl.pallas_call(kernel, out_shape=pltpu.VMEM((4, 512), F32), in_specs=spec...]
where the time goes in v6:
time: 63.4 us; the launch traced here: 62.9 us
  Pallas kernels  62.2 us (98%)
    pallas_call x1, Pallas kernels, on_device(): pl.pallas_call(kernel, out_shape=pltpu.VMEM((4, 512), F32), in_specs=spec...  62.2 us

profile of v6, /device:TPU:0, one launch (start us, length us, event | category | flops | bytes accessed | tf_op | source)
XLA Modules:
  0.0 62.9 jit_solution(13918837085236939336)
XLA Ops:
  0.0 62.2 %scores.1 = f32[4,512]{1,0:T(4,128)S(1)} custom-call(bf16[1024,512]{1,0:T(8,128)(2,1)} %bitcast.8, bf16[1024,4096]{1,0:T(8,128)(2,1)} %bitcast.6, bf16[1024,1792]{1,0:T(8,128)(2,1)} %bitcast.7, bf16[1792,256]{1,0:T(8,128)(2,1)} %w_hbm.1, s32[4]{0:T(128)} %len_ref.1, s32[8,512]{1,0:T(8,128)} %bitcast.10, s32[8,1792]{1,0:T(8,128)} %bitcast.9, f32[8,8]{1,0:T(8,128)} %bi_hbm.1, ...), custom_call_target="tpu_custom_call" | custom-call | flops 15032385536 | bytes 30000000 | tf_op jit(solution)/shard_map/scores/pallas_call | solution.py:562
  62.3 0.6 copy.13

commit v7 on v6

--- a/solution.py
+++ b/solution.py
@@ -22,73 +22,72 @@
 SCHEDULE = (
     (
         (
-            (0, 0, 0), (0, 1, 0), (0, 0, 1), (0, 1, 1), (0, 0, 2), (0, 1, 2), (0, 6, 0), (2, 0, 0),
+            (0, 0, 0), (0, 0, 1), (0, 0, 2), (0, 1, 0), (0, 1, 1), (0, 1, 2), (0, 6, 0), (2, 0, 0),
             (0, 2, 0), (0, 2, 1), (0, 2, 2), (0, 7, 0), (0, 7, 1), (2, 2, 0), (0, 0, 3), (0, 0, 4),
-            (0, 3, 2), (0, 6, 1), (0, 0, 5), (0, 0, 6), (2, 1, 0), (2, 3, 0), (0, 7, 4), (0, 7, 2),
-            (0, 1, 4), (0, 1, 3), (0, 2, 4), (0, 2, 3), (2, 5, 0), (0, 7, 5), (0, 6, 2), (1, 0, 0),
-            (0, 3, 1), (0, 3, 0), (0, 4, 2), (1, 0, 1), (2, 4, 0),
+            (0, 3, 2), (0, 6, 1), (0, 0, 5), (0, 0, 6), (2, 1, 0), (2, 3, 0), (0, 4, 2), (0, 7, 2),
+            (0, 1, 4), (0, 1, 3), (0, 2, 4), (0, 2, 3), (0, 5, 2), (2, 5, 0), (0, 3, 1), (0, 6, 2),
+            (1, 0, 0), (0, 3, 0), (0, 1, 8), (0, 1, 9), (0, 7, 4), (1, 0, 1), (2, 4, 0),
         ),
         (0, 0),
     ),
     (
         (
-            (0, 0, 7), (0, 0, 8), (0, 4, 1), (1, 1, 0), (0, 4, 0), (1, 2, 0), (0, 7, 6),
+            (0, 0, 7), (0, 4, 0), (0, 0, 8), (0, 4, 1), (1, 1, 0), (1, 2, 0), (0, 1, 7),
         ),
         (0, 1),
     ),
     (
         (
-            (0, 3, 3), (0, 5, 0), (0, 3, 4), (0, 5, 1), (0, 1, 7), (0, 7, 3),
+            (0, 3, 3), (0, 5, 0), (0, 3, 4), (0, 5, 1), (0, 2, 7), (0, 7, 3),
         ),
         (0, 2),
     ),
     (
         (
-            (0, 6, 3), (1, 0, 2), (0, 5, 2), (2, 6, 0), (0, 1, 6), (0, 1, 5),
+            (0, 6, 3), (1, 0, 2), (0, 1, 6), (0, 2, 8), (0, 1, 5), (2, 6, 0), (0, 2, 9), (0, 7, 5),
         ),
         (1, 0),
     ),
     (
         (
-            (0, 1, 8), (0, 1, 9), (1, 3, 0), (1, 6, 1), (1, 6, 2), (0, 4, 3), (0, 4, 4), (0, 2, 7),
-            (2, 7, 0), (0, 5, 3), (0, 5, 4), (1, 1, 2),
+            (0, 4, 3), (0, 4, 4), (1, 1, 2), (1, 3, 0), (1, 6, 1), (1, 6, 2), (0, 3, 7), (2, 7, 0),
+            (0, 5, 3), (0, 5, 4), (1, 2, 2),
         ),
         (0, 3),
     ),
     (
         (
-            (0, 2, 5), (0, 2, 6), (0, 7, 7), (1, 1, 1), (0, 3, 6), (0, 3, 5), (0, 2, 8), (0, 2, 9),
-            (0, 3, 7), (1, 4, 0),
+            (0, 2, 5), (0, 2, 6), (0, 7, 6), (1, 1, 1), (0, 3, 6), (0, 3, 5), (0, 7, 7), (1, 4, 0),
         ),
         (1, 1),
     ),
     (
         (
-            (1, 2, 2), (1, 5, 0), (0, 4, 6), (0, 4, 5),
+            (1, 5, 0), (0, 4, 6), (1, 3, 2), (0, 4, 5),
         ),
         (0, 4),
     ),
     (
         (
-            (0, 4, 7), (1, 6, 0),
+            (0, 4, 7), (1, 2, 1), (1, 6, 0),
         ),
         (0, 5),
     ),
     (
         (
-            (0, 5, 5), (0, 5, 6), (0, 5, 7), (1, 2, 1),
+            (0, 5, 5), (0, 5, 6), (0, 5, 7),
+        ),
+        (1, 2),
+    ),
+    (
+        (
+            (1, 3, 1),
         ),
         (2, 6),
     ),
     (
         (
-            (1, 3, 1), (1, 3, 2), (1, 4, 1),
-        ),
-        (1, 2),
-    ),
-    (
-        (
-            (1, 4, 2),
+            (1, 4, 1), (1, 4, 2),
         ),
         (1, 3),
     ),
@@ -194,7 +193,7 @@
 GIVE_FIRST = min(
     (i, n) for i, step in enumerate(PLAN) for n, (_, (what, at, which)) in enumerate(step) if (what, at) == (0, GATES) and which < 4
 )
-EARLY = [what == 0 and at == 0 and not new for new, (what, at, _) in PLAN[0]].index(False)
+EARLY = 3
 
 
 def column(slot):
@@ -298,7 +297,7 @@
     for i in range(1, 8):
         pl.semaphore_signal(barrier, inc=1, device_id=(dp, (tn + i) % 8), device_id_type=MESH)
     pl.semaphore_wait(barrier, 12)
-    loaded("own")
+    loaded("own", "plain")
 
     def remote(stage, i):
         if stage == GATES:
@@ -476,7 +475,6 @@
         for n, (arrivals, (what, at, which)) in enumerate(PLAN[i]):
             if i == 0 and n == EARLY:
                 start("give", "input", "insigns", "query", "signs", "c", "gate", "bi", "bo", "ev")
-                loaded("plain")
             for stage, copy in arrivals:
                 arrive(stage, copy)
             if what == 0:

time: 63.4 us -> 63.1 us (level)
  no operation moved by 1% of the time
where the time goes in v7:
time: 63.1 us; the launch traced here: 62.8 us
  Pallas kernels  62.2 us (99%)
    pallas_call x1, Pallas kernels, on_device(): pl.pallas_call(kernel, out_shape=pltpu.VMEM((4, 512), F32), in_specs=spec...  62.2 us

profile of v7, /device:TPU:0, one launch (start us, length us, event | category | flops | bytes accessed | tf_op | source)
XLA Modules:
  0.0 62.8 jit_solution(17551660026139507105)
XLA Ops:
  0.0 62.2 %scores.1 = f32[4,512]{1,0:T(4,128)S(1)} custom-call(bf16[1024,512]{1,0:T(8,128)(2,1)} %bitcast.8, bf16[1024,4096]{1,0:T(8,128)(2,1)} %bitcast.6, bf16[1024,1792]{1,0:T(8,128)(2,1)} %bitcast.7, bf16[1792,256]{1,0:T(8,128)(2,1)} %w_hbm.1, s32[4]{0:T(128)} %len_ref.1, s32[8,512]{1,0:T(8,128)} %bitcast.10, s32[8,1792]{1,0:T(8,128)} %bitcast.9, f32[8,8]{1,0:T(8,128)} %bi_hbm.1, ...), custom_call_target="tpu_custom_call" | custom-call | flops 15032385536 | bytes 30000000 | tf_op jit(solution)/shard_map/scores/pallas_call | solution.py:560
  62.2 0.6 copy.13

commit v8 on v7

--- a/solution.py
+++ b/solution.py
@@ -292,12 +292,13 @@
 
     start("own", "plain")
     barrier = pltpu.get_barrier_semaphore()
-    for name in ("xp", "xm", "z", "sib", "cross"):
+    for i in range(7):
+        peer = (dp, (zh + 1 - i // 4) % 2 * 4 + (y + FAR_FIRST[i % 4]) % 4)
+        pl.semaphore_signal(barrier, inc=1, device_id=peer, device_id_type=MESH)
+    for name in ("xp", "xm", "z", "cross", "sib"):
         pl.semaphore_signal(barrier, inc=1, device_id=dev[name], device_id_type=MESH)
-    for i in range(1, 8):
-        pl.semaphore_signal(barrier, inc=1, device_id=(dp, (tn + i) % 8), device_id_type=MESH)
     pl.semaphore_wait(barrier, 12)
-    loaded("own", "plain")
+    loaded("own")
 
     def remote(stage, i):
         if stage == GATES:
@@ -475,6 +476,7 @@
         for n, (arrivals, (what, at, which)) in enumerate(PLAN[i]):
             if i == 0 and n == EARLY:
                 start("give", "input", "insigns", "query", "signs", "c", "gate", "bi", "bo", "ev")
+                loaded("plain")
             for stage, copy in arrivals:
                 arrive(stage, copy)
             if what == 0:

time: 63.1 us -> 63.2 us (level)
  no operation moved by 1% of the time
where the time goes in v8:
time: 63.2 us; the launch traced here: 62.9 us
  Pallas kernels  62.3 us (99%)
    pallas_call x1, Pallas kernels, on_device(): pl.pallas_call(kernel, out_shape=pltpu.VMEM((4, 512), F32), in_specs=spec...  62.3 us

profile of v8, /device:TPU:0, one launch (start us, length us, event | category | flops | bytes accessed | tf_op | source)
XLA Modules:
  0.0 62.9 jit_solution(9777145851471363949)
XLA Ops:
  0.0 62.3 %scores.1 = f32[4,512]{1,0:T(4,128)S(1)} custom-call(bf16[1024,512]{1,0:T(8,128)(2,1)} %bitcast.8, bf16[1024,4096]{1,0:T(8,128)(2,1)} %bitcast.6, bf16[1024,1792]{1,0:T(8,128)(2,1)} %bitcast.7, bf16[1792,256]{1,0:T(8,128)(2,1)} %w_hbm.1, s32[4]{0:T(128)} %len_ref.1, s32[8,512]{1,0:T(8,128)} %bitcast.10, s32[8,1792]{1,0:T(8,128)} %bitcast.9, f32[8,8]{1,0:T(8,128)} %bi_hbm.1, ...), custom_call_target="tpu_custom_call" | custom-call | flops 15032385536 | bytes 30000000 | tf_op jit(solution)/shard_map/scores/pallas_call | solution.py:562
  62.3 0.6 copy.13

commit v9 on v7

--- a/solution.py
+++ b/solution.py
@@ -193,7 +193,7 @@
 GIVE_FIRST = min(
     (i, n) for i, step in enumerate(PLAN) for n, (_, (what, at, which)) in enumerate(step) if (what, at) == (0, GATES) and which < 4
 )
-EARLY = 3
+EARLY = 7
 
 
 def column(slot):

time: 63.1 us -> 63.1 us (level)
  no operation moved by 1% of the time
where the time goes in v9:
time: 63.1 us; the launch traced here: 62.9 us
  Pallas kernels  62.2 us (99%)
    pallas_call x1, Pallas kernels, on_device(): pl.pallas_call(kernel, out_shape=pltpu.VMEM((4, 512), F32), in_specs=spec...  62.2 us

profile of v9, /device:TPU:0, one launch (start us, length us, event | category | flops | bytes accessed | tf_op | source)
XLA Modules:
  0.0 62.9 jit_solution(4569007976149410359)
XLA Ops:
  0.0 62.2 %scores.1 = f32[4,512]{1,0:T(4,128)S(1)} custom-call(bf16[1024,512]{1,0:T(8,128)(2,1)} %bitcast.8, bf16[1024,4096]{1,0:T(8,128)(2,1)} %bitcast.6, bf16[1024,1792]{1,0:T(8,128)(2,1)} %bitcast.7, bf16[1792,256]{1,0:T(8,128)(2,1)} %w_hbm.1, s32[4]{0:T(128)} %len_ref.1, s32[8,512]{1,0:T(8,128)} %bitcast.10, s32[8,1792]{1,0:T(8,128)} %bitcast.9, f32[8,8]{1,0:T(8,128)} %bi_hbm.1, ...), custom_call_target="tpu_custom_call" | custom-call | flops 15032385536 | bytes 30000000 | tf_op jit(solution)/shard_map/scores/pallas_call | solution.py:560
  62.2 0.6 copy.13
